TPU v7x, 256 devices: a whole 4x4x8 slice. The times are simulated.
256 devices in a mesh: cont: 8 (over z), line: 8 (over y, core), scen: 4 (over x).
Axes of the slice: x: 4, y: 4, z: 8, core: 2. Of those that a mesh axis runs over, the one named last changes fastest.
Arguments:
- lodf: bfloat16 [1024, 4096], P('line', 'cont'), may hold values from -1 to 1
- flow: float32 [1024, 256], P('line', 'scen'), may hold values from -6 to 6
- out_flow: float32 [256, 4096], P('scen', 'cont'), may hold values from -6 to 6
- limits: float32 [1024], P('line'), may hold values from 0.5 to 2
- ptdf_mon: bfloat16 [1024, 2048], P('line'), may hold values from -6 to 6
- ptdf_out: bfloat16 [4096, 2048], P('cont'), may hold values from -6 to 6
- viol_cont: int32 [131072], P(('cont', 'line', 'scen')), may hold values from 0 to 511
- viol_line: int32 [131072], P(('cont', 'line', 'scen')), may hold values from 0 to 127
- viol_scen: int32 [131072], P(('cont', 'line', 'scen')), may hold values from 0 to 63
- rows_used: int32 [256], P(('cont', 'line', 'scen')), may hold values from 64 to 512, as said below
Outputs:
- worst: float32 [1024, 256], P('line', 'scen')
- schur: float32 [2048, 2048], P(('line', 'scen'))
Inputs may be any that keep to these rules, and one draw needn't show every extreme that they name: `rows_used`: each device uses a leading run of its 512 slots; the counts are skewed, and some device is full.
All inputs are finite; a program needn't handle non-finite values.
Results may differ from a plain program's by a relative error of at most 0.00096.
Values may be sent and summed in bfloat16 or wider, within the bound.
No kernel may reach another device: no remote copies, remote signals or barrier semaphores. Data moves between devices by JAX's collectives and lax.ppermute only.
A program may use at most 128 MiB of HBM per device.

v0:
```python
import math

import jax
import jax.numpy as jnp
from jax import lax
from jax.sharding import PartitionSpec as P


def local(
    lodf, flow, out_flow, limits, ptdf_mon, ptdf_out, viol_cont, viol_line, viol_scen, rows_used
):
    line_dev, cont_dev = lodf.shape
    scen_dev = flow.shape[1]
    width = ptdf_mon.shape[1]
    n_rows = viol_cont.shape[0]
    n_cont = lax.axis_size("cont")
    n_line = lax.axis_size("line")
    n_scen = lax.axis_size("scen")
    owners = n_line * n_scen
    devices = n_cont * owners
    row_block = math.gcd(n_rows, 512)
    lines_each = math.gcd(line_dev, 32)

    def screen(pair):
        lodf_block, flow_block = pair
        post = (
            flow_block[:, :, None]
            + lodf_block.astype(jnp.float32)[:, None, :] * out_flow[None, :, :]
        )
        return jnp.max(jnp.abs(post), axis=2)

    local_worst = lax.map(
        screen,
        (
            lodf.reshape(line_dev // lines_each, lines_each, cont_dev),
            flow.reshape(line_dev // lines_each, lines_each, scen_dev),
        ),
    ).reshape(line_dev, scen_dev)
    worst = lax.pmax(local_worst, "cont") / limits[:, None]
    coef = lodf[viol_line, viol_cont].astype(jnp.float32)
    rows = (
        ptdf_mon[viol_line].astype(jnp.float32)
        + coef[:, None] * ptdf_out[viol_cont].astype(jnp.float32)
    ).astype(jnp.bfloat16)
    rows = lax.optimization_barrier(rows)
    post = flow[viol_line, viol_scen] + coef * out_flow[viol_scen, viol_cont]
    ratio = post / limits[viol_line]
    live = jnp.arange(n_rows, dtype=jnp.int32) < rows_used[0]
    weight = jnp.where(live, 1.0 + ratio * ratio, jnp.zeros_like(ratio))
    scaled = (weight[:, None] * rows.astype(jnp.float32)).astype(jnp.bfloat16)
    trips = (rows_used[0] + row_block - 1) // row_block
    row_blocks = rows.reshape(n_rows // row_block, row_block, width)
    scaled_blocks = scaled.reshape(n_rows // row_block, row_block, width)

    def step(index, acc):
        row_tile = lax.dynamic_index_in_dim(row_blocks, index, 0, keepdims=False)
        scaled_tile = lax.dynamic_index_in_dim(scaled_blocks, index, 0, keepdims=False)
        return acc + lax.dot_general(
            row_tile, scaled_tile, (((0,), (0,)), ((), ())), preferred_element_type=jnp.float32
        )

    owned = lax.psum_scatter(
        lax.fori_loop(
            0,
            trips,
            step,
            jnp.zeros((lax.axis_size(("line", "scen")) * (width // owners), width), jnp.float32),
        ),
        ("line", "scen"),
        scatter_dimension=0,
        tiled=True,
    )
    total = lax.psum(owned, "cont")
    schur = total * (1.0 / (n_rows * devices))
    return (worst, schur)


def solution(mesh):
    in_specs = (
        P("line", "cont"),
        P("line", "scen"),
        P("scen", "cont"),
        P("line"),
        P("line", None),
        P("cont", None),
        P(("cont", "line", "scen")),
        P(("cont", "line", "scen")),
        P(("cont", "line", "scen")),
        P(("cont", "line", "scen")),
    )
    out_specs = (P("line", "scen"), P(("line", "scen"), None))
    return jax.shard_map(local, mesh=mesh, in_specs=in_specs, out_specs=out_specs, check_vma=False)
```

profile of v0, /device:TPU:1, one launch (start us, length us, event | category | flops | bytes accessed | tf_op | source)
XLA Modules:
  0.0 271.4 jit_solution(17831814919024099587)
XLA Ops:
  7.2 0.0 reduce-scatter.2.cloned.1.call-start
  8.1 0.7 shift-left_or_fusion
  8.8 5.2 %gather_fusion.1 = bf16[512]{0:T(512)(128)(2,1)S(1)} fusion(bf16[128,512]{1,0:T(8,128)(2,1)} %param.14, s32[512]{0:T(512)S(1)} %get-tuple-element.84), kind=kCustom, calls=%fused_computation.1 | custom fusion | bytes 6144 | tf_op jit(solution)/shard_map/gather | solution.py:40
  14.0 3.3 %gather_fusion = bf16[512,2048]{1,0:T(8,128)(2,1)} fusion(bf16[128,2048]{1,0:T(8,128)(2,1)S(1)} %copy-done.2, s32[1024]{0:T(1024)S(1)} %get-tuple-element.89), kind=kCustom, calls=%fused_computation | custom fusion | bytes 4196352 | tf_op jit(solution)/shard_map/gather | solution.py:42
  17.3 3.3 %gather_fusion.2 = bf16[512,2048]{1,0:T(8,128)(2,1)} fusion(bf16[512,2048]{1,0:T(8,128)(2,1)S(1)} %copy-done, s32[1024]{0:T(1024)S(1)} %get-tuple-element.88), kind=kCustom, calls=%fused_computation.2 | custom fusion | bytes 4196352 | tf_op jit(solution)/shard_map/gather | solution.py:43
  20.6 4.2 %add_convert_fusion = bf16[512,2048]{1,0:T(8,128)(2,1)} fusion(bf16[512,2048]{1,0:T(8,128)(2,1)} %gather_fusion.2, bf16[512,2048]{1,0:T(8,128)(2,1)} %gather_fusion, f32[512]{0:T(512)S(1)} %convert_element_type.36), kind=kLoop, calls=%fused_computation.14 | loop fusion | flops 5242880 | bytes 6293504 | tf_op jit(solution)/shard_map/convert_element_type | solution.py:44
  24.8 3.3 %gather_fusion.5 = f32[512]{0:T(512)S(1)} fusion(f32[128]{0:T(128)S(1)} %copy-done.1, s32[1024]{0:T(1024)S(1)} %get-tuple-element.89), kind=kCustom, calls=%fused_computation.5 | custom fusion | bytes 6144 | tf_op jit(solution)/shard_map/gather | solution.py:47
  28.2 3.7 %gather_fusion.3 = f32[512]{0:T(512)S(1)} fusion(f32[128,64]{0,1:T(8,128)S(1)} %copy-done.3, s32[512]{0:T(512)S(1)} %get-tuple-element.85), kind=kCustom, calls=%fused_computation.3 | custom fusion | bytes 8192 | tf_op jit(solution)/shard_map/gather | solution.py:46
  32.0 4.5 %gather_fusion.4 = f32[512]{0:T(512)S(1)} fusion(f32[64,512]{1,0:T(8,128)S(1)} %copy-done.4, s32[512]{0:T(512)S(1)} %get-tuple-element.83), kind=kCustom, calls=%fused_computation.4 | custom fusion | bytes 8192 | tf_op jit(solution)/shard_map/gather | solution.py:46
  36.5 3.3 %fusion.2 = bf16[1,512,2048]{2,1,0:T(8,128)(2,1)} fusion(bf16[512,2048]{1,0:T(8,128)(2,1)} %add_convert_fusion, f32[512]{0:T(512)S(1)} %add_select_fusion), kind=kLoop, calls=%fused_computation.15 | loop fusion | flops 3145728 | bytes 4196352 | tf_op jit(solution)/shard_map/reshape | solution.py:53
  39.8 7.9 %broadcast_in_dim.20 = f32[2048,2048]{1,0:T(8,128)} broadcast(f32[]{:T(128)} %constant.46.clone.1), dimensions={} | broadcast | bytes 16777220 | tf_op jit(solution)/shard_map/broadcast_in_dim | solution.py:67
  47.7 17.3 %while.21 = (s32[]{:T(128)}, f32[2048,2048]{1,0:T(8,128)}, s32[]{:T(128)}, bf16[1,512,2048]{2,1,0:T(8,128)(2,1)}, bf16[1,512,2048]{2,1,0:T(8,128)(2,1)}, /*index=5*/s32[]{:T(128)}) while((s32[]{:T(128)}, f32[2048,2048]{1,0:T(8,128)}, s32[]{:T(128)}, bf16[1,512,2048]{2,1,0:T(8,128)(2,1)}, bf16[1,512,2048]{2,1,0:T(8,128)(2,1)}, ...), condition=%wide.region_5.6_spmd, body=%wide.region_4.5_spmd.sunk | while | flops 4299161600 | bytes 37748804 | solution.py:63
  47.7 17.3 %convolution_add_fusion.2 = f32[2048,2048]{1,0:T(8,128)} fusion(f32[2048,2048]{1,0:T(8,128)} %get-tuple-element.178, bf16[1,512,2048]{2,1,0:T(8,128)(2,1)} %get-tuple-element.187, bf16[1,512,2048]{2,1,0:T(8,128)(2,1)} %get-tuple-element.186), kind=kOutput, calls=%fused_computation.10.clone.1 | convolution fusion | flops 4299161600 | bytes 37748736 | tf_op jit(solution)/shard_map/while/body/dot_general | solution.py:58
  65.1 0.0 reduce-scatter.2.cloned.1.call-update
  65.1 0.0 all-reduce.2.cloned.1.call-start
  65.1 0.1 copy.16
  65.2 125.2 %reduce-scatter.2.cloned.1.call-done = f32[64,2048]{1,0:T(8,128)} async-done(((f32[2048,2048]{1,0:T(8,128)}), f32[64,2048]{1,0:T(8,128)}) %reduce-scatter.2.cloned.1.call-update) | async-done | bytes 524304 | tf_op jit(solution)/shard_map/reduce_scatter | solution.py:62
  190.4 0.0 all-reduce.2.cloned.1.call-update
  190.5 7.2 %while.20 = (s32[]{:T(128)}, f32[4,32,64]{2,1,0:T(8,128)S(1)}, f32[4,32,64]{2,1,0:T(8,128)S(1)}, bf16[4,32,512]{2,1,0:T(8,128)(2,1)}, f32[64,512]{1,0:T(8,128)S(1)}, /*index=5*/s32[]{:T(128)}) while((s32[]{:T(128)}, f32[4,32,64]{2,1,0:T(8,128)S(1)}, f32[4,32,64]{2,1,0:T(8,128)S(1)}, bf16[4,32,512]{2,1,0:T(8,128)(2,1)}, ...), condition=%wide.region_2.3_spmd, body=%wide.region_0.2_spmd.sunk | while | flops 4208642 | bytes 360529 | solution.py:32
  190.5 0.8 bitcast_convert_fusion.2
  191.2 1.0 abs_reduce_fusion.2
  192.3 0.8 bitcast_convert_fusion.2
  193.0 1.0 abs_reduce_fusion.2
  194.1 0.8 bitcast_convert_fusion.2
  194.8 1.0 abs_reduce_fusion.2
  195.9 0.8 bitcast_convert_fusion.2
  196.6 1.0 abs_reduce_fusion.2
  197.6 24.7 %pmax.7 = f32[128,64]{1,0:T(8,128)S(1)} all-reduce(f32[128,64]{1,0:T(8,128)S(1)} %bitcast.35), channel_id=1, replica_groups=mesh['cont'=8,'line'=8,'scen'=4] {'cont'}, use_global_device_ids=true, to_apply=%region_3.4 | all-reduce | flops 8192 | bytes 65536 | tf_op jit(solution)/shard_map/pmax | solution.py:39
  222.3 0.1 broadcast_divide_fusion
  222.4 0.7 copy.17
  223.1 39.5 %all-reduce.2.cloned.1.call-done = f32[64,2048]{1,0:T(8,128)} async-done(((f32[64,2048]{1,0:T(8,128)}), f32[64,2048]{1,0:T(8,128)}) %all-reduce.2.cloned.1.call-update) | async-done | bytes 524304 | tf_op jit(solution)/shard_map/psum | solution.py:73
  262.7 1.9 broadcast_multiply_fusion
  (22 shorter events, 0.1 us)
Async XLA Ops:
  7.2 10.1 %copy-start = (bf16[512,2048]{1,0:T(8,128)(2,1)S(1)}, bf16[512,2048]{1,0:T(8,128)(2,1)}, u32[]{:S(2)}) copy-start(bf16[512,2048]{1,0:T(8,128)(2,1)} %param.19) | copy-start | bytes 6291460
  7.2 6.8 %copy-start.2 = (bf16[128,2048]{1,0:T(8,128)(2,1)S(1)}, bf16[128,2048]{1,0:T(8,128)(2,1)}, u32[]{:S(2)}) copy-start(bf16[128,2048]{1,0:T(8,128)(2,1)} %param.18) | copy-start | bytes 1572868
  7.2 183.2 %reduce-scatter.2.cloned.1.call-start = ((), (), s32[]{:S(2)}) async-start(), calls=%async_computation.1 | async-start | bytes 17301504 | tf_op jit(solution)/shard_map/reduce_scatter | solution.py:62
  20.6 4.2 %copy-start.1 = (f32[128]{0:T(128)S(1)}, f32[128]{0:T(128)}, u32[]{:S(2)}) copy-start(f32[128]{0:T(128)} %param.17) | copy-start | bytes 1540
  24.8 3.4 %copy-start.3 = (f32[128,64]{0,1:T(8,128)S(1)}, f32[128,64]{0,1:T(8,128)}, u32[]{:S(2)}) copy-start(f32[128,64]{0,1:T(8,128)} %param.15) | copy-start | bytes 98308
  24.8 7.1 %copy-start.4 = (f32[64,512]{1,0:T(8,128)S(1)}, f32[64,512]{1,0:T(8,128)}, u32[]{:S(2)}) copy-start(f32[64,512]{1,0:T(8,128)} %param.16) | copy-start | bytes 393220
  65.1 197.6 %all-reduce.2.cloned.1.call-start = ((), (), s32[]{:S(2)}) async-start(), calls=%async_computation.2 | async-start | bytes 1048576 | tf_op jit(solution)/shard_map/psum | solution.py:73
Sparse Core Ops, SparseCore 0:
  65.2 125.1 reduce-scatter.1
  192.8 69.8 all-reduce.1
where the time goes:
time: 276 us; the launch traced here: 271 us
  waiting for transfers between devices  165 us (60%)
  local copies, waits for them, and re-layouts  32.1 us (12%)
  blocking collectives  24.7 us (9%)
  other arithmetic  17.3 us (6%)
  matrix products  17.3 us (6%)
  between operations  15 us (5%)
    reduce_scatter x1, waiting for transfers between devices, local(): lax.psum_scatter(lax.fori_loop(0, trips, step, jnp.zeros((lax.axis_size((...  125 us
    psum x1, waiting for transfers between devices, local(): total = lax.psum(owned, 'cont')  39.5 us
    pmax x1, blocking collectives, local(): worst = lax.pmax(local_worst, 'cont') / limits[:, None]  24.7 us
    dot_general x1, matrix products, step(): lax.dot_general(row_tile, scaled_tile, (((0,), (0,)), ((), ())), preferre...  17.3 us
    gather x2, local copies, waits for them, and re-layouts, local(): post = flow[viol_line, viol_scen] + coef * out_flow[viol_scen, viol_cont]  8.27 us
    broadcast_in_dim x1, local copies, waits for them, and re-layouts, local(): jnp.zeros((lax.axis_size(('line', 'scen')) * (width // owners), width), j...  7.86 us
  transfers between devices with their start and end apart: 2, of which 2 were waited for; matrix products, arithmetic and copies ran while one was open for 3% of the time, Pallas kernels for 0%

commit v1 on v0

v1 whole, which is shorter than its diff:
```python
import functools

import jax
import jax.numpy as jnp
from jax import lax
from jax.experimental import pallas as pl
from jax.experimental.pallas import tpu as pltpu
from jax.sharding import PartitionSpec as P


F32 = jnp.float32
BF16 = jnp.bfloat16
VMEM_LIMIT = 48 * 1024 * 1024

M_OWN = 0
M_TILE = 16
LIST = 80
BLOCK1 = 112


def iota(shape, axis):
    return lax.broadcasted_iota(jnp.int32, shape, axis)


def dot(a, b, dims):
    return lax.dot_general(a, b, (dims, ((), ())), preferred_element_type=F32)


NN = ((1,), (0,))
NT = ((1,), (1,))
TN = ((0,), (0,))


def split(x):
    high = x.astype(BF16)
    return high, (x - high.astype(F32)).astype(BF16)


def split3(x):
    high = x.astype(BF16)
    rest = x - high.astype(F32)
    mid, low = split(rest)
    return high, mid, low


def prep_kernel(pos, used, lists, lodf, flow, out_flow, limits, mon, out):
    c, q = pos[0], pos[2]
    n = lists.shape[1]
    lines, conts = lodf.shape
    scens = flow.shape[0]
    k, l, s = lists[0:1, :], lists[1:2, :], lists[2:3, :]
    is_l = iota((lines, n), 0) == l
    is_s = iota((scens, n), 0) == s
    one_l = jnp.where(is_l, 1.0, 0.0).astype(BF16)
    one_k = jnp.where(iota((conts, n), 0) == k, 1.0, 0.0).astype(BF16)
    by_k = dot(jnp.concatenate([lodf[...], *split3(out_flow[...])], axis=0), one_k, NN)
    coef = jnp.sum(jnp.where(is_l, by_k[:lines], 0.0), axis=0, keepdims=True)
    outs = by_k[lines : lines + scens] + by_k[lines + scens : lines + 2 * scens]
    outs = outs + by_k[lines + 2 * scens :]
    outs = jnp.sum(jnp.where(is_s, outs, 0.0), axis=0, keepdims=True)
    ratings = jnp.broadcast_to(limits[...], (16, lines))
    by_l = dot(jnp.concatenate([*split3(flow[...]), *split3(ratings)], axis=0), one_l, NN)
    flows = by_l[:scens] + by_l[scens : 2 * scens] + by_l[2 * scens : 3 * scens]
    flows = jnp.sum(jnp.where(is_s, flows, 0.0), axis=0, keepdims=True)
    base = 3 * scens
    rating = by_l[base : base + 1] + by_l[base + 16 : base + 17] + by_l[base + 32 : base + 33]
    ratio = (flows + coef * outs) / rating
    weight = jnp.where(iota((1, n), 1) < used[0], 1.0 + ratio * ratio, 0.0)
    mixed = weight * coef
    square = mixed * coef

    def rows16(x):
        high, mid, low = split3(x)
        zero = jnp.zeros((5, n), F32)
        eight = jnp.concatenate(
            [high.astype(F32), mid.astype(F32), low.astype(F32), zero], axis=0
        )
        return jnp.concatenate([eight, jnp.zeros((8, n), F32)], axis=0).astype(BF16)

    e_parts = dot(rows16(square), one_k, NT)
    e_sum = e_parts[0:1] + e_parts[1:2] + e_parts[2:3]
    d_parts = dot(rows16(weight), one_l, NT)
    d_sum = d_parts[0:1] + d_parts[1:2] + d_parts[2:3]

    lf = l.astype(F32)
    kh = jnp.where(k >= conts // 2, 1.0, 0.0)
    kl = k.astype(F32) - kh * (conts // 2)
    fields = [lf, kh, kl, *[p.astype(F32) for p in split(mixed)], *[p.astype(F32) for p in split(e_sum)]]
    rows = [f[:, 128 * j : 128 * j + 128] for f in fields for j in range(4)]
    rows += [p.astype(F32) for p in split(d_sum)]
    second = jnp.where(used[0] > n // 2, 1.0, 0.0)
    rows += [jnp.full((1, 128), 1.0, F32) * second, jnp.zeros((1, 128), F32)]
    table = jnp.concatenate(rows, axis=0).astype(BF16)

    own = mon[pl.ds(pl.multiple_of(q * 32, 32), 32), :]
    for t in range(16):
        top, low = own[0:16, 128 * t : 128 * t + 128], own[16:32, 128 * t : 128 * t + 128]
        out[2 * t, M_OWN : M_OWN + 16, :] = jnp.concatenate([top[:, :64], low[:, :64]], axis=1)
        out[2 * t + 1, M_OWN : M_OWN + 16, :] = jnp.concatenate([top[:, 64:], low[:, 64:]], axis=1)
    for j in range(8):
        m = lax.rem(c - j + 8, 8)
        for r in range(4):
            out[m * 4 + r, M_TILE : M_TILE + 32, :] = own[:, 256 * j : 256 * j + 128]
            out[m * 4 + r, M_TILE + 32 : M_TILE + 64, :] = own[:, 256 * j + 128 : 256 * j + 256]
    for b in range(32):
        out[b, LIST : LIST + 32, :] = table


def own_columns(got, m):
    parts = []
    for r in range(4):
        piece = got[m * 4 + r, M_OWN : M_OWN + 16, :]
        parts += [piece[:, :64], piece[:, 64:]]
    return jnp.concatenate(parts, axis=0)


def product_kernel(pos, got, out_rows, out_own, screened, sent, acc, core):
    me = pos[1]
    acc[...] = jnp.zeros_like(acc)

    def table(m, r):
        return got[m * 4 + r, LIST : LIST + 32, :].astype(F32)

    def pieces(f, j):
        l, kh, kl, v = f[j : j + 1], f[4 + j : 5 + j], f[8 + j : 9 + j], f[12 + j : 13 + j]
        lane_l = iota((128, 128), 0).astype(F32) == l
        left = jnp.concatenate(
            [jnp.where(lane_l, v * (1.0 - kh), 0.0), jnp.where(lane_l, v * kh, 0.0)], axis=0
        ).astype(BF16)
        right = jnp.where(iota((256, 128), 0).astype(F32) == kl, 1.0, 0.0).astype(BF16)
        return left, right

    def block(m, sums):
        e_sum, d_all = sums
        tables = [table(m, r) for r in range(4)]
        both = [pieces(f, j) for f in tables for j in (0, 1)]
        core[...] = dot(
            jnp.concatenate([p[0] for p in both], axis=1),
            jnp.concatenate([p[1] for p in both], axis=1),
            NT,
        )
        for r in range(4):

            @pl.when(jnp.max(tables[r][30:31, :]) > 0.5)
            def _():
                late = [pieces(tables[r], j) for j in (2, 3)]
                core[...] += dot(
                    jnp.concatenate([p[0] for p in late], axis=1),
                    jnp.concatenate([p[1] for p in late], axis=1),
                    NT,
                )

        mon = own_columns(got, m)
        mon2 = jnp.concatenate([mon, mon], axis=0)
        for h in range(2):
            high, low = split(core[128 * h : 128 * h + 128, :])
            acc[:, 256 * h : 256 * h + 256] += dot(mon2, jnp.concatenate([high, low], axis=0), TN)
        total = tables[0] + tables[1] + tables[2] + tables[3]
        e_sum = e_sum + total[20:24] + total[24:28]
        d_row = total[28:29] + total[29:30]
        d_all = jnp.where(iota((8, 128), 0) == m, d_row, d_all)
        return e_sum, d_all

    e_sum, d_all = lax.fori_loop(
        0, 8, block, (jnp.zeros((4, 128), F32), jnp.zeros((8, 128), F32))
    )
    e_row = jnp.concatenate([e_sum[j : j + 1] for j in range(4)], axis=1)
    y = acc[...] + (0.5 * e_row) * out_own[...].astype(F32)
    left = jnp.concatenate(split(y), axis=0)
    d_high, d_low = [p.astype(F32) for p in split(d_all)]
    d_both = jnp.concatenate([d_high, d_low], axis=1)
    for j in range(8):
        both = dot(left, out_rows[:, 256 * j : 256 * j + 256], NN)
        sent[lax.rem(j + me, 8), 0:64, :] = (both[:64] + both[64:]).astype(BF16)
        w_high, w_low = [p.astype(F32) for p in split(screened[8 * j : 8 * j + 8, :])]
        w_both = jnp.concatenate([w_high, w_low], axis=1)
        sent[j, 64:80, :] = jnp.concatenate([w_both, d_both], axis=0).astype(BF16)


def combine_kernel(pos, got2, got, limits, turned, direct, worst):
    q = pos[2]
    a = got2[0, 0:64, :].astype(F32)
    tail = got2[0, 64:80, :].astype(F32)
    high = tail[0:8, :128] + tail[0:8, 128:]
    d_all = tail[8:16, :128] + tail[8:16, 128:]
    for i in range(1, 8):
        a = a + got2[i, 0:64, :].astype(F32)
        tail = got2[i, 64:80, :].astype(F32)
        high = jnp.maximum(high, tail[0:8, :128] + tail[0:8, 128:])
        d_all = d_all + (tail[8:16, :128] + tail[8:16, 128:])
    worst[...] = high / limits[...]
    for r in range(4):
        turned[lax.rem(r - q + 4, 4), :, :] = a[:, 64 * r : 64 * r + 64].T
    d_cols = d_all.T
    lefts, rights = [], []
    for m in range(8):
        scaled = own_columns(got, m).astype(F32) * d_cols[:, m : m + 1]
        lefts.append(jnp.concatenate(split(scaled), axis=1))
        for r in range(4):
            rights.append(
                jnp.concatenate(
                    [
                        got[m * 4 + r, M_TILE : M_TILE + 32, :],
                        got[m * 4 + r, M_TILE + 32 : M_TILE + 64, :],
                    ],
                    axis=1,
                )
            )
    both = dot(jnp.concatenate(lefts, axis=0), jnp.concatenate(rights, axis=0), TN)
    direct[...] = a + both[:64] + both[64:]


def finish_kernel(scale, pos, t0, t1, t2, t3, direct, worst, sent):
    q = pos[2]
    columns = []
    for r in range(4):
        j = lax.rem(q - r + 4, 4)
        columns.append(
            jnp.where(
                j == 0,
                t0[...],
                jnp.where(j == 1, t1[...], jnp.where(j == 2, t2[...], t3[...])),
            )
        )
    tile = (direct[...] + jnp.concatenate(columns, axis=1)) * scale
    tail = jnp.concatenate([worst[...], worst[...]], axis=1)
    for i in range(8):
        sent[i, 0:64, :] = tile
        sent[i, 64:72, :] = tail


def place_kernel(pos, got, schur, worst):
    me = pos[1]
    for j in range(8):
        schur[:, 256 * j : 256 * j + 256] = got[lax.rem(j + me, 8), 0:64, :]
        worst[8 * j : 8 * j + 8, :] = got[j, 64:72, 0:128]


def call(kernel, name, outs, *args, scalars=1, scratch=(), cost=None):
    vmem = pl.BlockSpec(memory_space=pltpu.VMEM)
    smem = pl.BlockSpec(memory_space=pltpu.SMEM)
    many = len(outs) > 1
    specs = [vmem] * len(outs)
    shapes = [jax.ShapeDtypeStruct(s, d) for s, d in outs]
    return pl.pallas_call(
        kernel,
        name=name,
        out_shape=shapes if many else shapes[0],
        in_specs=[smem] * scalars + [vmem] * (len(args) - scalars),
        out_specs=specs if many else specs[0],
        scratch_shapes=list(scratch),
        compiler_params=pltpu.CompilerParams(vmem_limit_bytes=VMEM_LIMIT),
        cost_estimate=cost,
    )(*args)


def local(
    lodf, flow, out_flow, limits, ptdf_mon, ptdf_out, viol_cont, viol_line, viol_scen, rows_used
):
    c, m, q = lax.axis_index("cont"), lax.axis_index("line"), lax.axis_index("scen")
    n_cont, n_line, n_scen = (lax.axis_size(a) for a in ("cont", "line", "scen"))
    n_rows = viol_cont.shape[0]
    scale = 1.0 / (n_rows * n_cont * n_line * n_scen)
    pos = jnp.stack([c, m, q]).astype(jnp.int32)
    lists = jnp.stack([viol_cont, viol_line, viol_scen])
    ratings = limits.reshape(1, -1)
    flow_t = flow.T

    block1 = call(
        prep_kernel,
        "prep",
        [((32, BLOCK1, 128), BF16)],
        pos, rows_used, lists, lodf, flow_t, out_flow, ratings, ptdf_mon,
        scalars=2,
    )
    got1 = lax.all_to_all(block1, ("line", "scen"), 0, 0, tiled=True)

    wide = lodf.astype(F32)
    terms = wide[None, :, :] * out_flow[:, None, :]
    screened = jnp.maximum(
        jnp.abs(flow_t + jnp.max(terms, axis=2)), jnp.abs(flow_t + jnp.min(terms, axis=2))
    )
    own = lax.dynamic_slice_in_dim(ptdf_out, (m * n_scen + q) * 64, 64, 1).T

    block2 = call(
        product_kernel,
        "product",
        [((8, 80, 256), BF16)],
        pos, got1, ptdf_out, own, screened,
        scratch=[pltpu.VMEM((64, 512), F32), pltpu.VMEM((256, 256), F32)],
    )
    got2 = lax.all_to_all(block2, "cont", 0, 0, tiled=True)
    turned, direct, worst_part = call(
        combine_kernel,
        "combine",
        [((4, 64, 64), F32), ((64, 256), F32), ((8, 128), F32)],
        pos, got2, got1, ratings,
    )

    def place(i, j, k):
        return (i * n_line + j) * n_scen + k

    swapped = []
    for step in range(4):
        pairs = [
            (place(i, j, k), place(i, (i - j) % 8, (k + step) % 4))
            for i in range(n_cont)
            for j in range(n_line)
            for k in range(n_scen)
        ]
        swapped.append(lax.ppermute(turned[step], ("cont", "line", "scen"), pairs))
    block3 = call(
        functools.partial(finish_kernel, scale),
        "finish",
        [((8, 72, 256), F32)],
        pos, *swapped, direct, worst_part,
    )
    got3 = lax.all_to_all(block3, "cont", 0, 0, tiled=True)
    schur, worst_t = call(
        place_kernel, "place", [((64, 2048), F32), ((64, 128), F32)], pos, got3
    )
    return worst_t.T, schur


def solution(mesh):
    in_specs = (
        P("line", "cont"),
        P("line", "scen"),
        P("scen", "cont"),
        P("line"),
        P("line", None),
        P("cont", None),
        P(("cont", "line", "scen")),
        P(("cont", "line", "scen")),
        P(("cont", "line", "scen")),
        P(("cont", "line", "scen")),
    )
    out_specs = (P("line", "scen"), P(("line", "scen"), None))
    return jax.shard_map(local, mesh=mesh, in_specs=in_specs, out_specs=out_specs, check_vma=False)
```

time: 276 us -> 102 us (0.37)
  the two profiles are of different devices: /device:TPU:1 before, /device:TPU:2 now
where the time goes in v1:
time: 102 us; the launch traced here: 101 us
  blocking collectives  50 us (49%)
  Pallas kernels  15.3 us (15%)
  starting transfers between devices  13.1 us (13%)
  waiting for transfers between devices  11.3 us (11%)
  other arithmetic  5.07 us (5%)
  local copies, waits for them, and re-layouts  4.5 us (4%)
  between operations  1.56 us (2%)
    all_to_all x1, blocking collectives, local(): got3 = lax.all_to_all(block3, 'cont', 0, 0, tiled=True)  28.3 us
    all_to_all x1, blocking collectives, local(): got2 = lax.all_to_all(block2, 'cont', 0, 0, tiled=True)  21.7 us
    pallas_call x5, Pallas kernels, call(): pl.pallas_call(kernel, name=name, out_shape=shapes if many else shapes[0]...  15.3 us
    all_to_all x1, waiting for transfers between devices, local(): got1 = lax.all_to_all(block1, ('line', 'scen'), 0, 0, tiled=True)  8.76 us
    all_to_all x1, starting transfers between devices, local(): got1 = lax.all_to_all(block1, ('line', 'scen'), 0, 0, tiled=True)  7.62 us
    ppermute x4, starting transfers between devices, local(): swapped.append(lax.ppermute(turned[step], ('cont', 'line', 'scen'), pairs))  5.52 us
    unnamed x21, local copies, waits for them, and re-layouts  4.38 us
    reduce_max x1, other arithmetic, local(): jnp.max(terms, axis=2)  3.52 us
  transfers between devices with their start and end apart: 5, of which 3 were waited for; matrix products, arithmetic and copies ran while one was open for 4% of the time, Pallas kernels for 0%

profile of v1, /device:TPU:2, one launch (start us, length us, event | category | flops | bytes accessed | tf_op | source)
XLA Modules:
  0.0 100.9 jit_solution(2822134066084320346)
XLA Ops:
  1.4 0.1 pad_add_fusion.1.pos
  1.5 0.7 pad_add_fusion.lists
  2.2 0.0 copy-start.1
  2.3 0.9 copy-done.1
  3.2 0.9 copy-done.3
  4.1 1.0 %copy-done.5 = bf16[128,2048]{1,0:T(8,128)(2,1)S(1)} copy-done((bf16[128,2048]{1,0:T(8,128)(2,1)S(1)}, bf16[128,2048]{1,0:T(8,128)(2,1)}, u32[]{:S(2)}) %copy-start.5) | copy-done | bytes 524312
  5.1 0.8 copy-done.6
  5.9 0.7 copy-done.8
  6.5 2.2 %prep.1 = bf16[32,112,128]{2,1,0:T(8,128)(2,1)} custom-call(s32[3]{0:T(128)S(1)} %pad_add_fusion.1.pos, s32[1]{0:T(128)S(6)} %copy.15.used, s32[3,512]{1,0:T(4,128)S(1)} %pad_add_fusion.lists, bf16[128,512]{1,0:T(8,128)(2,1)S(1)} %copy-done.1, f32[64,128]{1,0:T(8,128)S(1)} %bitcast.20, f32[64,512]{1,0:T(8,128)S(1)} %copy-done.3, f32[1,128]{1,0:T(1,128)S(1)} %bitcast.21, ...), custom_call_target="tpu_custom_call" | custom-call | tf_op jit(solution)/shard_map/prep/pallas_call | solution.py:245
  8.8 7.6 %all-to-all-start = ((bf16[32,112,128]{2,1,0:T(8,128)(2,1)}), bf16[32,112,128]{2,1,0:T(8,128)(2,1)S(1)}, u32[]{:S(2)}, u32[]{:S(2)}) async-start(bf16[32,112,128]{2,1,0:T(8,128)(2,1)} %prep.1), calls=%async_computation | async-start | bytes 1835008 | tf_op jit(solution)/shard_map/all_to_all | solution.py:276
  16.4 0.0 copy-done.2
  16.4 0.7 convert_element_type.3
  17.1 0.0 copy-done
  17.1 0.1 constant_dynamic-slice_fusion
  17.2 0.1 copy.14
  17.4 3.5 %multiply_reduce_fusion.1 = (f32[64,128]{1,0:T(8,128)S(1)}, f32[64,128]{1,0:T(8,128)S(1)}) fusion(f32[64,512]{1,0:T(8,128)S(1)} %copy-done.4, f32[128,512]{1,0:T(8,128)} %convert_element_type.3), kind=kLoop, calls=%fused_computation.1 | loop fusion | flops 12566528 | bytes 458752 | tf_op jit(solution)/shard_map/reduce_max | solution.py:281
  20.9 0.0 copy-start.9
  20.9 8.8 %all-to-all-done.got = bf16[32,112,128]{2,1,0:T(8,128)(2,1)S(1)} async-done(((bf16[32,112,128]{2,1,0:T(8,128)(2,1)}), bf16[32,112,128]{2,1,0:T(8,128)(2,1)S(1)}, u32[]{:S(2)}, u32[]{:S(2)}) %all-to-all-start) | async-done | bytes 917536 | tf_op jit(solution)/shard_map/all_to_all | solution.py:276
  29.7 9.5 %product.1 = bf16[8,80,256]{2,1,0:T(8,128)(2,1)S(1)} custom-call(s32[3]{0:T(128)S(1)} %pad_add_fusion.1.pos, bf16[32,112,128]{2,1,0:T(8,128)(2,1)S(1)} %all-to-all-done.got, bf16[512,2048]{1,0:T(8,128)(2,1)S(1)} %copy-done, bf16[64,512]{1,0:T(8,128)(2,1)S(1)} %bitcast.19, f32[64,128]{1,0:T(8,128)S(1)} %abs_maximum_fusion.screened), custom_call_target="tpu_custom_call" | custom-call | tf_op jit(solution)/shard_map/product/pallas_call | solution.py:245
  39.2 21.7 %all_to_all.15.got2 = bf16[8,80,256]{2,1,0:T(8,128)(2,1)S(1)} all-to-all(bf16[8,80,256]{2,1,0:T(8,128)(2,1)S(1)} %product.1), channel_id=1, replica_groups=mesh['cont'=8,'line'=8,'scen'=4] {'cont'}, dimensions={0} | all-to-all | bytes 655360 | tf_op jit(solution)/shard_map/all_to_all | solution.py:292
  60.9 1.5 %combine.1 = (f32[4,64,64]{2,1,0:T(8,128)S(1)}, f32[64,256]{1,0:T(8,128)S(1)}, f32[8,128]{1,0:T(8,128)S(1)}) custom-call(s32[3]{0:T(128)S(1)} %pad_add_fusion.1.pos, bf16[8,80,256]{2,1,0:T(8,128)(2,1)S(1)} %all_to_all.15.got2, bf16[32,112,128]{2,1,0:T(8,128)(2,1)S(1)} %all-to-all-done.got, f32[1,128]{1,0:T(1,128)S(1)} %bitcast.22), custom_call_target="tpu_custom_call" | custom-call | tf_op jit(solution)/shard_map/combine/pallas_call | solution.py:245
  62.4 0.7 collective-permute-start
  63.1 1.5 %collective-permute-start.1 = (f32[64,64]{1,0:T(8,128)S(1)}, f32[64,64]{1,0:T(8,128)S(1)}, u32[]{:S(2)}, u32[]{:S(2)}) collective-permute-start(f32[64,64]{1,0:T(8,128)S(1)} %get-tuple-element.16), channel_id=1, source_target_pairs={{0,1},{1,2},{2,3},{3,0},{4,29},{5,30},{6,31},{7,28},{8,25},{9,26},... | collective-permute-start | bytes 49160 | tf_op jit(solution)/shard_map/ppermute | solution.py:311
  64.5 2.1 %collective-permute-start.2 = (f32[64,64]{1,0:T(8,128)S(1)}, f32[64,64]{1,0:T(8,128)S(1)}, u32[]{:S(2)}, u32[]{:S(2)}) collective-permute-start(f32[64,64]{1,0:T(8,128)S(1)} %get-tuple-element.15), channel_id=1, source_target_pairs={{0,2},{1,3},{2,0},{3,1},{4,30},{5,31},{6,28},{7,29},{8,26},{9,27},... | collective-permute-start | bytes 49160 | tf_op jit(solution)/shard_map/ppermute | solution.py:311
  66.6 1.3 %collective-permute-start.3 = (f32[64,64]{1,0:T(8,128)S(1)}, f32[64,64]{1,0:T(8,128)S(1)}, u32[]{:S(2)}, u32[]{:S(2)}) collective-permute-start(f32[64,64]{1,0:T(8,128)S(1)} %get-tuple-element.14), channel_id=1, source_target_pairs={{0,3},{1,0},{2,1},{3,2},{4,31},{5,28},{6,29},{7,30},{8,27},{9,24},... | collective-permute-start | bytes 49160 | tf_op jit(solution)/shard_map/ppermute | solution.py:311
  67.9 0.0 collective-permute-done.t0
  67.9 0.0 collective-permute-done.1.t1
  68.0 2.0 %collective-permute-done.2.t2 = f32[64,64]{1,0:T(8,128)S(1)} collective-permute-done((f32[64,64]{1,0:T(8,128)S(1)}, f32[64,64]{1,0:T(8,128)S(1)}, u32[]{:S(2)}, u32[]{:S(2)}) %collective-permute-start.2) | collective-permute-done | bytes 16416 | tf_op jit(solution)/shard_map/ppermute | solution.py:311
  70.0 0.5 collective-permute-done.3.t3
  70.5 0.7 finish.1
  71.2 28.3 %all_to_all.16.got = f32[8,72,256]{2,1,0:T(8,128)S(1)} all-to-all(f32[8,72,256]{2,1,0:T(8,128)S(1)} %finish.1), channel_id=1, replica_groups=mesh['cont'=8,'line'=8,'scen'=4] {'cont'}, dimensions={0} | all-to-all | bytes 1179648 | tf_op jit(solution)/shard_map/all_to_all | solution.py:318
  99.5 1.4 %place.1 = (f32[64,2048]{1,0:T(8,128)}, f32[64,128]{1,0:T(8,128)}) custom-call(s32[3]{0:T(128)S(1)} %pad_add_fusion.1.pos, f32[8,72,256]{2,1,0:T(8,128)S(1)} %all_to_all.16.got), custom_call_target="tpu_custom_call" | custom-call | tf_op jit(solution)/shard_map/place/pallas_call | solution.py:245
  (13 shorter events, 0.0 us)
Async XLA Ops:
  0.6 16.5 %copy-start = (bf16[512,2048]{1,0:T(8,128)(2,1)S(1)}, bf16[512,2048]{1,0:T(8,128)(2,1)}, u32[]{:S(2)}) copy-start(bf16[512,2048]{1,0:T(8,128)(2,1)} %out_rows.1) | copy-start | bytes 6291460
  2.2 0.9 copy-start.1
  3.2 0.9 copy-start.3
  4.1 1.0 %copy-start.5 = (bf16[128,2048]{1,0:T(8,128)(2,1)S(1)}, bf16[128,2048]{1,0:T(8,128)(2,1)}, u32[]{:S(2)}) copy-start(bf16[128,2048]{1,0:T(8,128)(2,1)} %mon.1) | copy-start | bytes 1572868
  5.1 0.8 copy-start.6
  5.9 0.7 copy-start.8
  6.5 9.9 %copy-start.2 = (bf16[128,512]{1,0:T(8,128)(2,1)S(1)}, bf16[128,512]{1,0:T(8,128)(2,1)}, u32[]{:S(2)}) copy-start(bf16[128,512]{1,0:T(8,128)(2,1)} %lodf.1) | copy-start | bytes 393220
  6.5 10.8 %copy-start.4 = (f32[64,512]{1,0:T(8,128)S(1)}, f32[64,512]{1,0:T(8,128)}, u32[]{:S(2)}) copy-start(f32[64,512]{1,0:T(8,128)} %out_flow.1) | copy-start | bytes 393220
  6.5 14.4 %copy-start.7 = (f32[128,64]{0,1:T(8,128)S(1)}, f32[128,64]{0,1:T(8,128)}, u32[]{:S(2)}) copy-start(f32[128,64]{0,1:T(8,128)} %param.11) | copy-start | bytes 98308
  8.8 20.9 %all-to-all-start = ((bf16[32,112,128]{2,1,0:T(8,128)(2,1)}), bf16[32,112,128]{2,1,0:T(8,128)(2,1)S(1)}, u32[]{:S(2)}, u32[]{:S(2)}) async-start(bf16[32,112,128]{2,1,0:T(8,128)(2,1)} %prep.1), calls=%async_computation | async-start | bytes 1835008 | tf_op jit(solution)/shard_map/all_to_all | solution.py:276
  20.9 40.0 %copy-start.9 = (f32[128]{0:T(128)S(1)}, f32[128]{0:T(128)}, u32[]{:S(2)}) copy-start(f32[128]{0:T(128)} %param.13) | copy-start | bytes 1540
  62.4 5.5 %collective-permute-start = (f32[64,64]{1,0:T(8,128)S(1)}, f32[64,64]{1,0:T(8,128)S(1)}, u32[]{:S(2)}, u32[]{:S(2)}) collective-permute-start(f32[64,64]{1,0:T(8,128)S(1)} %get-tuple-element.17), channel_id=1, source_target_pairs={{0,0},{1,1},{2,2},{3,3},{4,28},{5,29},{6,30},{7,31},{8,24},{9,25},... | collective-permute-start | bytes 49160 | tf_op jit(solution)/shard_map/ppermute | solution.py:311
  63.1 4.9 %collective-permute-start.1 = (f32[64,64]{1,0:T(8,128)S(1)}, f32[64,64]{1,0:T(8,128)S(1)}, u32[]{:S(2)}, u32[]{:S(2)}) collective-permute-start(f32[64,64]{1,0:T(8,128)S(1)} %get-tuple-element.16), channel_id=1, source_target_pairs={{0,1},{1,2},{2,3},{3,0},{4,29},{5,30},{6,31},{7,28},{8,25},{9,26},... | collective-permute-start | bytes 49160 | tf_op jit(solution)/shard_map/ppermute | solution.py:311
  64.5 5.4 %collective-permute-start.2 = (f32[64,64]{1,0:T(8,128)S(1)}, f32[64,64]{1,0:T(8,128)S(1)}, u32[]{:S(2)}, u32[]{:S(2)}) collective-permute-start(f32[64,64]{1,0:T(8,128)S(1)} %get-tuple-element.15), channel_id=1, source_target_pairs={{0,2},{1,3},{2,0},{3,1},{4,30},{5,31},{6,28},{7,29},{8,26},{9,27},... | collective-permute-start | bytes 49160 | tf_op jit(solution)/shard_map/ppermute | solution.py:311
  66.6 3.9 %collective-permute-start.3 = (f32[64,64]{1,0:T(8,128)S(1)}, f32[64,64]{1,0:T(8,128)S(1)}, u32[]{:S(2)}, u32[]{:S(2)}) collective-permute-start(f32[64,64]{1,0:T(8,128)S(1)} %get-tuple-element.14), channel_id=1, source_target_pairs={{0,3},{1,0},{2,1},{3,2},{4,31},{5,28},{6,29},{7,30},{8,27},{9,24},... | collective-permute-start | bytes 49160 | tf_op jit(solution)/shard_map/ppermute | solution.py:311

commit v2 on v1

v2 whole, which is shorter than its diff:
```python
import functools

import jax
import jax.numpy as jnp
from jax import lax
from jax.experimental import pallas as pl
from jax.experimental.pallas import tpu as pltpu
from jax.sharding import Mesh
from jax.sharding import PartitionSpec as P


F32 = jnp.float32
BF16 = jnp.bfloat16
I16 = jnp.int16

M_OWN = 0
M_TILE = 32
LIST = 64
BLOCK1 = 96

TAIL2 = 128
BLOCK2 = 160

BLOCK3 = 80


def iota(shape, axis):
    return lax.broadcasted_iota(jnp.int32, shape, axis)


def dot(a, b, dims):
    return lax.dot_general(a, b, (dims, ((), ())), preferred_element_type=F32)


NN = ((1,), (0,))
NT = ((1,), (1,))
TN = ((0,), (0,))


def split(x):
    high = x.astype(BF16)
    return high, (x - high.astype(F32)).astype(BF16)


def split3(x):
    high = x.astype(BF16)
    rest = x - high.astype(F32)
    mid, low = split(rest)
    return high, mid, low


def place():
    return tuple(lax.axis_index(a) for a in ("cont", "y", "core", "scen"))


def prep_kernel(*refs):
    hbm, out, local, sems = refs[:9], refs[9], refs[10:19], refs[19]
    c, y, core, q = place()
    lines_here = pl.ds(pl.multiple_of(q * 32, 32), 32)
    copies = []
    for i, (source, target) in enumerate(zip(hbm, local)):
        source = source.at[lines_here, :] if i == 8 else source
        copies.append(pltpu.make_async_copy(source, target, sems.at[i]))
    for copy in copies:
        copy.start()
    for copy in copies[:8]:
        copy.wait()
    used, k4, l4, s4, lodf, flow, out_flow, limits, own_ref = local
    n = 512

    def row(ref):
        return jnp.concatenate([ref[j : j + 1, :] for j in range(4)], axis=1)

    k, l, s = row(k4), row(l4), row(s4)
    lines, conts = lodf.shape
    scens = flow.shape[0]
    is_l = iota((lines, n), 0) == l
    is_s = iota((scens, n), 0) == s
    one_l = jnp.where(is_l, 1.0, 0.0).astype(BF16)
    one_k = jnp.where(iota((conts, n), 0) == k, 1.0, 0.0).astype(BF16)
    by_k = dot(jnp.concatenate([lodf[...], *split3(out_flow[...])], axis=0), one_k, NN)
    coef = jnp.sum(jnp.where(is_l, by_k[:lines], 0.0), axis=0, keepdims=True)
    outs = by_k[lines : lines + scens] + by_k[lines + scens : lines + 2 * scens]
    outs = outs + by_k[lines + 2 * scens :]
    outs = jnp.sum(jnp.where(is_s, outs, 0.0), axis=0, keepdims=True)
    ratings = jnp.broadcast_to(limits[...], (16, lines))
    by_l = dot(jnp.concatenate([*split3(flow[...]), *split3(ratings)], axis=0), one_l, NN)
    flows = by_l[:scens] + by_l[scens : 2 * scens] + by_l[2 * scens : 3 * scens]
    flows = jnp.sum(jnp.where(is_s, flows, 0.0), axis=0, keepdims=True)
    base = 3 * scens
    rating = by_l[base : base + 1] + by_l[base + 16 : base + 17] + by_l[base + 32 : base + 33]
    ratio = (flows + coef * outs) / rating
    weight = jnp.where(iota((1, n), 1) < used[0], 1.0 + ratio * ratio, 0.0)
    mixed = weight * coef
    square = mixed * coef

    def rows16(x):
        parts = [p.astype(F32) for p in split3(x)]
        return jnp.concatenate([*parts, jnp.zeros((13, n), F32)], axis=0).astype(BF16)

    e_parts = dot(rows16(square), one_k, NT)
    e_sum = e_parts[0:1] + e_parts[1:2] + e_parts[2:3]
    d_parts = dot(rows16(weight), one_l, NT)
    d_sum = d_parts[0:1] + d_parts[1:2] + d_parts[2:3]

    upper = k >= conts // 2
    kl = jnp.where(upper, k - conts // 2, k)
    fields = [
        l.astype(F32),
        kl.astype(F32),
        jnp.where(upper, 0.0, mixed),
        jnp.where(upper, mixed, 0.0),
        *[p.astype(F32) for p in split(e_sum)],
    ]
    rows = [f[:, 128 * j : 128 * j + 128] for f in fields for j in range(4)]
    rows += [p.astype(F32) for p in split(d_sum)]
    rows += [jnp.full((1, 128), jnp.where(used[0] > n // 2, 1.0, 0.0), F32)]
    rows += [jnp.zeros((32 - len(rows), 128), F32)]
    table = jnp.concatenate(rows, axis=0).astype(BF16)
    for b in range(32):
        out[b, LIST : LIST + 32, :] = table

    copies[8].wait()
    own = own_ref[...]
    t_y, t_q = core * 2 + c // 4, c % 4
    for yy in range(4):
        for qq in range(4):
            first = 512 * yy + 64 * qq
            part = jnp.concatenate(
                [own[:, first : first + 64], own[:, first + 256 : first + 320]], axis=1
            )
            for cc in range(2):
                out[(yy * 2 + cc) * 4 + qq, M_OWN : M_OWN + 32, :] = part
                to_y = lax.bitwise_xor(jnp.int32(yy), 2 * cc + c // 4)
                to_q = lax.bitwise_xor(jnp.int32(qq), t_q)
                out[(to_y * 2 + cc) * 4 + to_q, M_TILE : M_TILE + 32, :] = part


def product_kernel(got, out_rows, own_t, screened, sent, acc, core_ref):
    c, y, core, q = place()
    acc[...] = jnp.zeros_like(acc)

    def pieces(f, j):
        l, kl, low, up = f[j : j + 1], f[4 + j : 5 + j], f[8 + j : 9 + j], f[12 + j : 13 + j]
        is_l = iota((128, 128), 0).astype(F32) == l
        left = jnp.concatenate(
            [jnp.where(is_l, low, 0.0), jnp.where(is_l, up, 0.0)], axis=0
        ).astype(BF16)
        right = jnp.where(iota((256, 128), 0).astype(F32) == kl, 1.0, 0.0).astype(BF16)
        return left, right

    def pair(parts):
        return (
            jnp.concatenate([p[0] for p in parts], axis=1),
            jnp.concatenate([p[1] for p in parts], axis=1),
        )

    def block(m, sums):
        e_sum, d_all = sums
        tables = [got[m * 4 + r, LIST : LIST + 32, :].astype(F32) for r in range(4)]
        core_ref[...] = dot(*pair([pieces(f, j) for f in tables for j in (0, 1)]), NT)
        for r in range(4):

            @pl.when(jnp.max(tables[r][26:27, :]) > 0.5)
            def _():
                core_ref[...] += dot(*pair([pieces(tables[r], j) for j in (2, 3)]), NT)

        mon = jnp.concatenate([got[m * 4 + r, M_OWN : M_OWN + 32, :] for r in range(4)], axis=0)
        mon2 = jnp.concatenate([mon, mon], axis=0)
        for h in range(2):
            high, low = split(core_ref[128 * h : 128 * h + 128, :])
            acc[:, 256 * h : 256 * h + 256] += dot(mon2, jnp.concatenate([high, low], axis=0), TN)
        total = tables[0] + tables[1] + tables[2] + tables[3]
        e_sum = e_sum + total[16:20] + total[20:24]
        d_all = jnp.where(iota((8, 128), 0) == m, total[24:25] + total[25:26], d_all)
        return e_sum, d_all

    e_sum, d_all = lax.fori_loop(
        0, 8, block, (jnp.zeros((4, 128), F32), jnp.zeros((8, 128), F32))
    )
    e_row = jnp.concatenate([e_sum[j : j + 1] for j in range(4)], axis=1)
    part = acc[...] + (0.5 * e_row) * own_t[...].astype(F32)
    left = jnp.concatenate(split(part), axis=0)
    d_rows = [p.astype(F32) for p in split(d_all)]
    for i in range(8):
        w_rows = [p.astype(F32) for p in split(screened[8 * i : 8 * i + 8, :])]
        sent[i, TAIL2:BLOCK2, :] = jnp.concatenate([*w_rows, *d_rows], axis=0).astype(BF16)
    half = lax.bitwise_xor(y // 2, core)
    columns = out_rows[:, pl.ds(pl.multiple_of(half * 1024, 1024), 1024)]
    for yy in range(2):
        both = dot(left, columns[:, 512 * yy : 512 * yy + 512], NN)
        tile = (both[:128] + both[128:]).astype(BF16)
        for qq in range(4):
            to = lax.bitwise_xor(jnp.int32(yy), y % 2) * 4 + lax.bitwise_xor(jnp.int32(qq), q)
            sent[to, 0:128, :] = jnp.concatenate(
                [tile[:, 64 * qq : 64 * qq + 64], tile[:, 256 + 64 * qq : 320 + 64 * qq]], axis=1
            )


def combine_kernel(got2, got, limits, turned, direct, worst):
    a = got2[0, 0:128, :].astype(F32)
    tail = got2[0, TAIL2:BLOCK2, :].astype(F32)
    high = tail[0:8] + tail[8:16]
    d_all = tail[16:24] + tail[24:32]
    for i in range(1, 8):
        a = a + got2[i, 0:128, :].astype(F32)
        tail = got2[i, TAIL2:BLOCK2, :].astype(F32)
        high = jnp.maximum(high, tail[0:8] + tail[8:16])
        d_all = d_all + (tail[16:24] + tail[24:32])
    worst[...] = high / limits[...]
    turned[...] = a.T
    d_cols = d_all.T
    lefts, rights = [], []
    for m in range(8):
        mon = jnp.concatenate([got[m * 4 + r, M_OWN : M_OWN + 32, :] for r in range(4)], axis=0)
        lefts.append(jnp.concatenate(split(mon.astype(F32) * d_cols[:, m : m + 1]), axis=1))
        rights += [got[m * 4 + r, M_TILE : M_TILE + 32, :] for r in range(4)]
    both = dot(jnp.concatenate(lefts, axis=0), jnp.concatenate(rights, axis=0), TN)
    direct[...] = a + both[:128] + both[128:]


def encode(x):
    top = jnp.maximum(jnp.max(jnp.abs(x), axis=0, keepdims=True), 1e-30)
    exponent = jnp.floor(jnp.log2(top) + 1.001) - 15.0
    return jnp.floor(x * jnp.exp2(-exponent) + 0.5), exponent


def finish_kernel(scale, turned, direct, worst, sent):
    tile = (direct[...] + turned[...]) * scale
    worst_code, worst_exp = encode(worst[...])
    for core in range(2):
        code, exp = encode(tile[64 * core : 64 * core + 64, :])
        rows = [code, worst_code, exp, worst_exp, jnp.zeros((BLOCK3 - 74, 128), F32)]
        block = jnp.concatenate(rows, axis=0).astype(jnp.int32).astype(I16)
        for i in range(8):
            sent[2 * i + core, :, :] = block


def decode(code, exponent):
    return code * jnp.exp2(exponent)


def place_kernel(got, schur, worst):
    c, y, core, q = place()
    for yy in range(4):
        parts = []
        for qq in range(4):
            source_c = lax.bitwise_xor(jnp.int32(yy % 2), y % 2) * 4
            source_c = source_c + lax.bitwise_xor(jnp.int32(qq), q)
            source_core = lax.bitwise_xor(jnp.int32(yy // 2), y // 2)
            block = got[source_c * 2 + source_core, :, :].astype(jnp.int32).astype(F32)
            parts.append(decode(block[0:64], block[72:73]))
        schur[:, 512 * yy : 512 * yy + 512] = jnp.concatenate(
            [p[:, :64] for p in parts] + [p[:, 64:] for p in parts], axis=1
        )
    for i in range(8):
        block = got[2 * i + core, 64:80, :].astype(jnp.int32).astype(F32)
        worst[8 * i : 8 * i + 8, :] = decode(block[0:8], block[9:10])


def call(kernel, name, outs, *args, scratch=(), space=pltpu.VMEM, vmem_mib=24):
    vmem = pl.BlockSpec(memory_space=pltpu.VMEM)
    specs = [vmem] * len(outs)
    shapes = [jax.ShapeDtypeStruct(s, d) for s, d in outs]
    many = len(outs) > 1
    return pl.pallas_call(
        kernel,
        name=name,
        out_shape=shapes if many else shapes[0],
        in_specs=[pl.BlockSpec(memory_space=space)] * len(args),
        out_specs=specs if many else specs[0],
        scratch_shapes=list(scratch),
        compiler_params=pltpu.CompilerParams(vmem_limit_bytes=vmem_mib * 1024 * 1024),
    )(*args)


PLANE = ("y", "core", "scen")
EVERY = ("cont", "y", "core", "scen")


def local(
    lodf, flow, out_flow, limits, ptdf_mon, ptdf_out, viol_cont, viol_line, viol_scen, rows_used
):
    sizes = [lax.axis_size(a) for a in EVERY]
    n_rows = viol_cont.shape[0]
    scale = 1.0 / (n_rows * sizes[0] * sizes[1] * sizes[2] * sizes[3])
    ratings = limits.reshape(1, -1)
    flow_t = flow.T

    inputs = [
        rows_used,
        viol_cont.reshape(4, 128),
        viol_line.reshape(4, 128),
        viol_scen.reshape(4, 128),
        lodf,
        flow_t,
        out_flow,
        ratings,
        ptdf_mon,
    ]
    scratch = [pltpu.SMEM(rows_used.shape, jnp.int32)]
    scratch += [pltpu.VMEM(a.shape, a.dtype) for a in inputs[1:8]]
    scratch += [pltpu.VMEM((32, ptdf_mon.shape[1]), BF16), pltpu.SemaphoreType.DMA((9,))]
    block1 = call(
        prep_kernel, "prep", [((32, BLOCK1, 128), BF16)], *inputs, scratch=scratch, space=pl.ANY, vmem_mib=60
    )
    got1 = lax.all_to_all(block1, PLANE, 0, 0, tiled=True)

    wide = lodf.astype(F32)
    terms = wide[None, :, :] * out_flow[:, None, :]
    screened = jnp.maximum(
        jnp.abs(flow_t + jnp.max(terms, axis=2)), jnp.abs(flow_t + jnp.min(terms, axis=2))
    )
    first = 512 * lax.axis_index("y") + 64 * lax.axis_index("scen")
    own_t = jnp.concatenate(
        [lax.dynamic_slice_in_dim(ptdf_out, first + 256 * i, 64, 1) for i in range(2)], axis=1
    ).T

    block2 = call(
        product_kernel,
        "product",
        [((8, BLOCK2, 128), BF16)],
        got1, ptdf_out, own_t, screened,
        scratch=[pltpu.VMEM((128, 512), F32), pltpu.VMEM((256, 256), F32)],
    )
    got2 = lax.all_to_all(block2, "cont", 0, 0, tiled=True)
    turned, direct, worst_part = call(
        combine_kernel,
        "combine",
        [((128, 128), F32), ((128, 128), F32), ((8, 128), F32)],
        got2, got1, ratings,
    )

    def index(c, y, core, q):
        return ((c * sizes[1] + y) * sizes[2] + core) * sizes[3] + q

    pairs = [
        (index(c, y, core, q), index(c, y ^ (core * 2 + c // 4), core, q ^ (c % 4)))
        for c in range(sizes[0])
        for y in range(sizes[1])
        for core in range(sizes[2])
        for q in range(sizes[3])
    ]
    turned = lax.ppermute(turned, EVERY, pairs)
    block3 = call(
        functools.partial(finish_kernel, scale),
        "finish",
        [((16, BLOCK3, 128), I16)],
        turned, direct, worst_part,
    )
    got3 = lax.all_to_all(block3, ("cont", "core"), 0, 0, tiled=True)
    schur, worst_t = call(
        place_kernel, "place", [((64, 2048), F32), ((64, 128), F32)], got3
    )
    return worst_t.T, schur


def solution(mesh):
    n_cont, n_line, n_scen = (mesh.shape[a] for a in ("cont", "line", "scen"))
    fine = Mesh(mesh.devices.reshape(n_cont, n_line // 2, 2, n_scen), EVERY)
    line = ("y", "core")
    every = P(EVERY)
    in_specs = (
        P(line, "cont"),
        P(line, "scen"),
        P("scen", "cont"),
        P(line),
        P(line, None),
        P("cont", None),
        every,
        every,
        every,
        every,
    )
    out_specs = (P(line, "scen"), P((*line, "scen"), None))
    return jax.shard_map(local, mesh=fine, in_specs=in_specs, out_specs=out_specs, check_vma=False)
```

time: 102 us -> 83.4 us (0.82)
  the two profiles are of different devices: /device:TPU:2 before, /device:TPU:1 now
where the time goes in v2:
time: 83.4 us; the launch traced here: 83.1 us
  blocking collectives  39.1 us (47%)
  starting transfers between devices  13.8 us (17%)
  Pallas kernels  13.4 us (16%)
  waiting for transfers between devices  10.1 us (12%)
  other arithmetic  4.19 us (5%)
  between operations  1.57 us (2%)
  local copies, waits for them, and re-layouts  0.99 us (1%)
    all_to_all x1, blocking collectives, local(): got2 = lax.all_to_all(block2, 'cont', 0, 0, tiled=True)  19.8 us
    all_to_all x1, blocking collectives, local(): got3 = lax.all_to_all(block3, ('cont', 'core'), 0, 0, tiled=True)  19.3 us
    pallas_call x5, Pallas kernels, call(): pl.pallas_call(kernel, name=name, out_shape=shapes if many else shapes[0]...  13.4 us
    all_to_all x1, starting transfers between devices, local(): got1 = lax.all_to_all(block1, PLANE, 0, 0, tiled=True)  8.6 us
    all_to_all x1, waiting for transfers between devices, local(): got1 = lax.all_to_all(block1, PLANE, 0, 0, tiled=True)  8.42 us
    ppermute x1, starting transfers between devices, local(): turned = lax.ppermute(turned, EVERY, pairs)  5.23 us
    reduce_max x1, other arithmetic, local(): jnp.max(terms, axis=2)  2.54 us
  transfers between devices with their start and end apart: 2, of which 2 were waited for; matrix products, arithmetic and copies ran while one was open for 6% of the time, Pallas kernels for 0%

profile of v2, /device:TPU:1, one launch (start us, length us, event | category | flops | bytes accessed | tf_op | source)
XLA Modules:
  0.0 83.1 jit_solution(10089340329643101333)
XLA Ops:
  0.6 0.0 copy-start.2
  0.6 0.0 copy-start
  1.4 0.0 copy-start.3
  1.5 2.9 %prep.1 = bf16[32,96,128]{2,1,0:T(8,128)(2,1)} custom-call(s32[1]{0:T(128)S(6)} %copy.18.refs_0_, s32[4,128]{1,0:T(4,128)} %bitcast.12, s32[4,128]{1,0:T(4,128)} %bitcast.13, s32[4,128]{1,0:T(4,128)} %bitcast.14, bf16[128,512]{1,0:T(8,128)(2,1)} %refs_4_.1, f32[64,128]{1,0:T(8,128)} %bitcast.11, f32[64,512]{1,0:T(8,128)} %refs_6_.1, f32[1,128]{1,0:T(1,128)} %bitcast.9, ...), custom_call_target="tpu_custom_call" | custom-call | tf_op jit(solution)/shard_map/prep/pallas_call | solution.py:266
  4.4 8.6 %all-to-all-start = ((bf16[32,96,128]{2,1,0:T(8,128)(2,1)}), bf16[32,96,128]{2,1,0:T(8,128)(2,1)S(1)}, u32[]{:S(2)}, u32[]{:S(2)}) async-start(bf16[32,96,128]{2,1,0:T(8,128)(2,1)} %prep.1), calls=%async_computation | async-start | bytes 1572864 | tf_op jit(solution)/shard_map/all_to_all | solution.py:307
  13.0 0.0 copy-done.2
  13.1 0.0 copy-done
  13.1 0.1 constant_dynamic-slice_fusion.1
  13.2 0.7 copy.17
  14.0 0.1 copy.16
  14.1 0.9 %maximum_bitcast_fusion.own_t = bf16[128,512]{1,0:T(8,128)(2,1)S(1)} fusion(bf16[512,64]{0,1:T(8,128)(2,1)} %copy.17, bf16[512,64]{0,1:T(8,128)(2,1)S(1)} %copy.16), kind=kLoop, calls=%fused_computation.2 | loop fusion | flops 262144 | bytes 262144 | tf_op jit(solution)/shard_map/transpose | solution.py:317
  14.9 0.0 copy-done.3
  14.9 2.5 %multiply_reduce_fusion.1 = (f32[64,128]{1,0:T(8,128)S(1)}, f32[64,128]{1,0:T(8,128)S(1)}) fusion(f32[64,512]{1,0:T(8,128)S(1)} %copy-done.3, f32[128,512]{1,0:T(8,128)S(1)} %convert_element_type.3), kind=kLoop, calls=%fused_computation.1 | loop fusion | flops 12566528 | bytes 458752 | tf_op jit(solution)/shard_map/reduce_max | solution.py:312
  17.5 0.0 copy-start.1
  17.5 0.8 abs_maximum_fusion.screened
  18.3 8.4 %all-to-all-done.got = bf16[32,96,128]{2,1,0:T(8,128)(2,1)S(1)} async-done(((bf16[32,96,128]{2,1,0:T(8,128)(2,1)}), bf16[32,96,128]{2,1,0:T(8,128)(2,1)S(1)}, u32[]{:S(2)}, u32[]{:S(2)}) %all-to-all-start) | async-done | bytes 786464 | tf_op jit(solution)/shard_map/all_to_all | solution.py:307
  26.7 8.7 %product.1 = bf16[8,160,128]{2,1,0:T(8,128)(2,1)S(1)} custom-call(bf16[32,96,128]{2,1,0:T(8,128)(2,1)S(1)} %all-to-all-done.got, bf16[512,2048]{1,0:T(8,128)(2,1)S(1)} %copy-done, bf16[128,512]{1,0:T(8,128)(2,1)S(1)} %maximum_bitcast_fusion.own_t, f32[64,128]{1,0:T(8,128)S(1)} %abs_maximum_fusion.screened), custom_call_target="tpu_custom_call" | custom-call | tf_op jit(solution)/shard_map/product/pallas_call | solution.py:266
  35.4 19.8 %all_to_all.15.got2 = bf16[8,160,128]{2,1,0:T(8,128)(2,1)S(1)} all-to-all(bf16[8,160,128]{2,1,0:T(8,128)(2,1)S(1)} %product.1), channel_id=1, replica_groups=mesh['cont'=8,'y'=4,'core'=2,'scen'=4] {'cont'}, dimensions={0} | all-to-all | bytes 655360 | tf_op jit(solution)/shard_map/all_to_all | solution.py:326
  55.2 0.0 copy-done.1
  55.2 0.6 combine.1
  55.8 5.2 %collective-permute-start = (f32[128,128]{1,0:T(8,128)S(1)}, f32[128,128]{1,0:T(8,128)S(1)}, u32[]{:S(2)}, u32[]{:S(2)}) collective-permute-start(f32[128,128]{1,0:T(8,128)S(1)} %get-tuple-element.7), channel_id=1, source_target_pairs={{0,0},{1,1},{2,2},{3,3},{4,20},{5,21},{6,22},{7,23},{8,8},{9,9},{1... | collective-permute-start | bytes 196616 | tf_op jit(solution)/shard_map/ppermute | solution.py:344
  61.1 1.6 %collective-permute-done.turned = f32[128,128]{1,0:T(8,128)S(1)} collective-permute-done((f32[128,128]{1,0:T(8,128)S(1)}, f32[128,128]{1,0:T(8,128)S(1)}, u32[]{:S(2)}, u32[]{:S(2)}) %collective-permute-start) | collective-permute-done | bytes 65568 | tf_op jit(solution)/shard_map/ppermute | solution.py:344
  62.7 0.1 finish.1
  62.8 19.3 %all_to_all.16.got = s16[16,80,128]{2,1,0:T(8,128)(2,1)S(1)} all-to-all(s16[16,80,128]{2,1,0:T(8,128)(2,1)S(1)} %finish.1), channel_id=1, replica_groups=mesh['cont'=8,'y'=4,'core'=2,'scen'=4] {'cont','core'}, dimensions={0} | all-to-all | bytes 655360 | tf_op jit(solution)/shard_map/all_to_all | solution.py:351
  82.1 1.0 %place.1 = (f32[64,2048]{1,0:T(8,128)}, f32[64,128]{1,0:T(8,128)}) custom-call(s16[16,80,128]{2,1,0:T(8,128)(2,1)S(1)} %all_to_all.16.got), custom_call_target="tpu_custom_call" | custom-call | tf_op jit(solution)/shard_map/place/pallas_call | solution.py:266
  (1 shorter events, 0.0 us)
Async XLA Ops:
  0.6 12.4 %copy-start.2 = (bf16[128,512]{1,0:T(8,128)(2,1)S(1)}, bf16[128,512]{1,0:T(8,128)(2,1)}, u32[]{:S(2)}) copy-start(bf16[128,512]{1,0:T(8,128)(2,1)} %refs_4_.1) | copy-start | bytes 393220
  0.6 12.4 %copy-start = (bf16[512,2048]{1,0:T(8,128)(2,1)S(1)}, bf16[512,2048]{1,0:T(8,128)(2,1)}, u32[]{:S(2)}) copy-start(bf16[512,2048]{1,0:T(8,128)(2,1)} %out_rows.1) | copy-start | bytes 6291460
  1.4 13.5 %copy-start.3 = (f32[64,512]{1,0:T(8,128)S(1)}, f32[64,512]{1,0:T(8,128)}, u32[]{:S(2)}) copy-start(f32[64,512]{1,0:T(8,128)} %refs_6_.1) | copy-start | bytes 393220
  4.4 22.3 %all-to-all-start = ((bf16[32,96,128]{2,1,0:T(8,128)(2,1)}), bf16[32,96,128]{2,1,0:T(8,128)(2,1)S(1)}, u32[]{:S(2)}, u32[]{:S(2)}) async-start(bf16[32,96,128]{2,1,0:T(8,128)(2,1)} %prep.1), calls=%async_computation | async-start | bytes 1572864 | tf_op jit(solution)/shard_map/all_to_all | solution.py:307
  17.5 37.7 %copy-start.1 = (f32[128]{0:T(128)S(1)}, f32[128]{0:T(128)}, u32[]{:S(2)}) copy-start(f32[128]{0:T(128)} %param.13) | copy-start | bytes 1540
  55.8 6.9 %collective-permute-start = (f32[128,128]{1,0:T(8,128)S(1)}, f32[128,128]{1,0:T(8,128)S(1)}, u32[]{:S(2)}, u32[]{:S(2)}) collective-permute-start(f32[128,128]{1,0:T(8,128)S(1)} %get-tuple-element.7), channel_id=1, source_target_pairs={{0,0},{1,1},{2,2},{3,3},{4,20},{5,21},{6,22},{7,23},{8,8},{9,9},{1... | collective-permute-start | bytes 196616 | tf_op jit(solution)/shard_map/ppermute | solution.py:344

commit v3 on v2

--- a/solution.py
+++ b/solution.py
@@ -63,7 +63,7 @@
         copies.append(pltpu.make_async_copy(source, target, sems.at[i]))
     for copy in copies:
         copy.start()
-    for copy in copies[:8]:
+    for copy in copies:
         copy.wait()
     used, k4, l4, s4, lodf, flow, out_flow, limits, own_ref = local
     n = 512
@@ -114,32 +114,28 @@
     ]
     rows = [f[:, 128 * j : 128 * j + 128] for f in fields for j in range(4)]
     rows += [p.astype(F32) for p in split(d_sum)]
-    rows += [jnp.full((1, 128), jnp.where(used[0] > n // 2, 1.0, 0.0), F32)]
     rows += [jnp.zeros((32 - len(rows), 128), F32)]
     table = jnp.concatenate(rows, axis=0).astype(BF16)
-    for b in range(32):
+    for b in range(16):
         out[b, LIST : LIST + 32, :] = table
 
-    copies[8].wait()
     own = own_ref[...]
-    t_y, t_q = core * 2 + c // 4, c % 4
     for yy in range(4):
         for qq in range(4):
             first = 512 * yy + 64 * qq
             part = jnp.concatenate(
                 [own[:, first : first + 64], own[:, first + 256 : first + 320]], axis=1
             )
+            out[yy * 4 + qq, M_OWN : M_OWN + 32, :] = part
             for cc in range(2):
-                out[(yy * 2 + cc) * 4 + qq, M_OWN : M_OWN + 32, :] = part
                 to_y = lax.bitwise_xor(jnp.int32(yy), 2 * cc + c // 4)
-                to_q = lax.bitwise_xor(jnp.int32(qq), t_q)
-                out[(to_y * 2 + cc) * 4 + to_q, M_TILE : M_TILE + 32, :] = part
-
-
-def product_kernel(got, out_rows, own_t, screened, sent, acc, core_ref):
-    c, y, core, q = place()
-    acc[...] = jnp.zeros_like(acc)
-
+                to = to_y * 4 + lax.bitwise_xor(jnp.int32(qq), c % 4)
+                lines = jnp.where(to < yy * 4 + qq, part[0:16].astype(F32), part[16:32].astype(F32))
+                first_row = M_TILE + 16 * cc
+                out[to, first_row : first_row + 16, :] = lines.astype(BF16)
+
+
+def half_product(got):
     def pieces(f, j):
         l, kl, low, up = f[j : j + 1], f[4 + j : 5 + j], f[8 + j : 9 + j], f[12 + j : 13 + j]
         is_l = iota((128, 128), 0).astype(F32) == l
@@ -149,46 +145,45 @@
         right = jnp.where(iota((256, 128), 0).astype(F32) == kl, 1.0, 0.0).astype(BF16)
         return left, right
 
-    def pair(parts):
-        return (
-            jnp.concatenate([p[0] for p in parts], axis=1),
-            jnp.concatenate([p[1] for p in parts], axis=1),
+    e_sum, d_rows, cores = jnp.zeros((8, 128), F32), [], []
+    for yy in range(4):
+        tables = [got[yy * 4 + r, LIST : LIST + 32, :].astype(F32) for r in range(4)]
+        both = [pieces(f, j) for f in tables for j in range(4)]
+        core = dot(
+            jnp.concatenate([p[0] for p in both], axis=1),
+            jnp.concatenate([p[1] for p in both], axis=1),
+            NT,
         )
-
-    def block(m, sums):
-        e_sum, d_all = sums
-        tables = [got[m * 4 + r, LIST : LIST + 32, :].astype(F32) for r in range(4)]
-        core_ref[...] = dot(*pair([pieces(f, j) for f in tables for j in (0, 1)]), NT)
-        for r in range(4):
-
-            @pl.when(jnp.max(tables[r][26:27, :]) > 0.5)
-            def _():
-                core_ref[...] += dot(*pair([pieces(tables[r], j) for j in (2, 3)]), NT)
-
-        mon = jnp.concatenate([got[m * 4 + r, M_OWN : M_OWN + 32, :] for r in range(4)], axis=0)
-        mon2 = jnp.concatenate([mon, mon], axis=0)
-        for h in range(2):
-            high, low = split(core_ref[128 * h : 128 * h + 128, :])
-            acc[:, 256 * h : 256 * h + 256] += dot(mon2, jnp.concatenate([high, low], axis=0), TN)
+        cores.append(jnp.concatenate([core[:128], core[128:]], axis=1))
         total = tables[0] + tables[1] + tables[2] + tables[3]
-        e_sum = e_sum + total[16:20] + total[20:24]
-        d_all = jnp.where(iota((8, 128), 0) == m, total[24:25] + total[25:26], d_all)
-        return e_sum, d_all
-
-    e_sum, d_all = lax.fori_loop(
-        0, 8, block, (jnp.zeros((4, 128), F32), jnp.zeros((8, 128), F32))
-    )
+        e_sum = e_sum + total[16:24]
+        d_rows.append(total[24:25] + total[25:26])
+    mon = jnp.concatenate([got[i, M_OWN : M_OWN + 32, :] for i in range(16)], axis=0)
+    high, low = split(jnp.concatenate(cores, axis=0))
+    part = dot(mon, high, TN) + dot(mon, low, TN)
+    return part, jnp.concatenate([e_sum[0:4] + e_sum[4:8], *d_rows], axis=0)
+
+
+def first_kernel(got, part, sums):
+    part[...], sums[...] = half_product(got)
+
+
+def second_kernel(got, part1, sums1, out_rows, own_t, screened, sent):
+    c, y, core, q = place()
+    part, sums = half_product(got)
+    e_sum = sums1[0:4, :] + sums[0:4]
     e_row = jnp.concatenate([e_sum[j : j + 1] for j in range(4)], axis=1)
-    part = acc[...] + (0.5 * e_row) * own_t[...].astype(F32)
+    part = part1[...] + part + (0.5 * e_row) * own_t[...].astype(F32)
     left = jnp.concatenate(split(part), axis=0)
+    d_all = jnp.concatenate([sums1[4:8, :], sums[4:8]], axis=0)
     d_rows = [p.astype(F32) for p in split(d_all)]
     for i in range(8):
         w_rows = [p.astype(F32) for p in split(screened[8 * i : 8 * i + 8, :])]
         sent[i, TAIL2:BLOCK2, :] = jnp.concatenate([*w_rows, *d_rows], axis=0).astype(BF16)
     half = lax.bitwise_xor(y // 2, core)
-    columns = out_rows[:, pl.ds(pl.multiple_of(half * 1024, 1024), 1024)]
     for yy in range(2):
-        both = dot(left, columns[:, 512 * yy : 512 * yy + 512], NN)
+        first = pl.multiple_of(half * 1024 + 512 * yy, 512)
+        both = dot(left, out_rows[:, pl.ds(first, 512)], NN)
         tile = (both[:128] + both[128:]).astype(BF16)
         for qq in range(4):
             to = lax.bitwise_xor(jnp.int32(yy), y % 2) * 4 + lax.bitwise_xor(jnp.int32(qq), q)
@@ -197,7 +192,8 @@
             )
 
 
-def combine_kernel(got2, got, limits, turned, direct, worst):
+def combine_kernel(got2, own, other, limits, turned, direct, worst, d_ref):
+    c, y, core, q = place()
     a = got2[0, 0:128, :].astype(F32)
     tail = got2[0, TAIL2:BLOCK2, :].astype(F32)
     high = tail[0:8] + tail[8:16]
@@ -208,15 +204,42 @@
         high = jnp.maximum(high, tail[0:8] + tail[8:16])
         d_all = d_all + (tail[16:24] + tail[24:32])
     worst[...] = high / limits[...]
-    turned[...] = a.T
-    d_cols = d_all.T
-    lefts, rights = [], []
-    for m in range(8):
-        mon = jnp.concatenate([got[m * 4 + r, M_OWN : M_OWN + 32, :] for r in range(4)], axis=0)
-        lefts.append(jnp.concatenate(split(mon.astype(F32) * d_cols[:, m : m + 1]), axis=1))
-        rights += [got[m * 4 + r, M_TILE : M_TILE + 32, :] for r in range(4)]
-    both = dot(jnp.concatenate(lefts, axis=0), jnp.concatenate(rights, axis=0), TN)
-    direct[...] = a + both[:128] + both[128:]
+    d_ref[...] = d_all.T
+
+    def side(h):
+        lefts = []
+        for i, got in enumerate((own, other)):
+            for yy in range(4):
+                for r in range(4):
+                    lines = pl.ds(pl.multiple_of(32 * r + 16 * h, 16), 16)
+                    mon = got[yy * 4 + r, pl.ds(pl.multiple_of(M_OWN + 16 * h, 16), 16), :]
+                    scaled = mon.astype(F32) * d_ref[lines, 4 * i + yy : 4 * i + yy + 1]
+                    lefts.append(jnp.concatenate(split(scaled), axis=1))
+        return jnp.concatenate(lefts, axis=0)
+
+    def write(both, factor):
+        total = a + factor * (both[:128] + both[128:])
+        direct[...] = total
+        turned[...] = total.T
+
+    alone = (c == 0) & (core == 0)
+
+    @pl.when(alone)
+    def _():
+        both = 0.0
+        for h in range(2):
+            rights = [g[i, M_OWN + 16 * h : M_OWN + 16 * h + 16, :] for g in (own, other) for i in range(16)]
+            both = both + dot(side(h), jnp.concatenate(rights, axis=0), TN)
+        write(both, 0.5)
+
+    @pl.when(jnp.logical_not(alone))
+    def _():
+        to_y = lax.bitwise_xor(y, 2 * core + c // 4)
+        to_q = lax.bitwise_xor(q, c % 4)
+        h = jnp.where(y * 4 + q < to_y * 4 + to_q, 0, 1)
+        there = pl.ds(pl.multiple_of(M_TILE + 16 * core, 16), 16)
+        rights = [g[i, there, :] for g in (own, other) for i in range(16)]
+        write(dot(side(h), jnp.concatenate(rights, axis=0), TN), 1.0)
 
 
 def encode(x):
@@ -274,7 +297,6 @@
     )(*args)
 
 
-PLANE = ("y", "core", "scen")
 EVERY = ("cont", "y", "core", "scen")
 
 
@@ -302,9 +324,10 @@
     scratch += [pltpu.VMEM(a.shape, a.dtype) for a in inputs[1:8]]
     scratch += [pltpu.VMEM((32, ptdf_mon.shape[1]), BF16), pltpu.SemaphoreType.DMA((9,))]
     block1 = call(
-        prep_kernel, "prep", [((32, BLOCK1, 128), BF16)], *inputs, scratch=scratch, space=pl.ANY, vmem_mib=60
-    )
-    got1 = lax.all_to_all(block1, PLANE, 0, 0, tiled=True)
+        prep_kernel, "prep", [((16, BLOCK1, 128), BF16)], *inputs, scratch=scratch, space=pl.ANY, vmem_mib=60
+    )
+    got1 = lax.all_to_all(block1, ("y", "scen"), 0, 0, tiled=True)
+    other1 = lax.ppermute(got1, "core", [(0, 1), (1, 0)])
 
     wide = lodf.astype(F32)
     terms = wide[None, :, :] * out_flow[:, None, :]
@@ -316,19 +339,20 @@
         [lax.dynamic_slice_in_dim(ptdf_out, first + 256 * i, 64, 1) for i in range(2)], axis=1
     ).T
 
+    part, sums = call(first_kernel, "first", [((128, 512), F32), ((8, 128), F32)], got1)
     block2 = call(
-        product_kernel,
-        "product",
+        second_kernel,
+        "second",
         [((8, BLOCK2, 128), BF16)],
-        got1, ptdf_out, own_t, screened,
-        scratch=[pltpu.VMEM((128, 512), F32), pltpu.VMEM((256, 256), F32)],
+        other1, part, sums, ptdf_out, own_t, screened,
     )
     got2 = lax.all_to_all(block2, "cont", 0, 0, tiled=True)
     turned, direct, worst_part = call(
         combine_kernel,
         "combine",
         [((128, 128), F32), ((128, 128), F32), ((8, 128), F32)],
-        got2, got1, ratings,
+        got2, got1, other1, ratings,
+        scratch=[pltpu.VMEM((128, 8), F32)],
     )
 
     def index(c, y, core, q):

time: 83.4 us -> 74.2 us (0.89)
  Pallas kernels: 13.4 us -> 7.96 us
  starting transfers between devices: 13.8 us -> 11.9 us
  other arithmetic: 4.19 us -> 2.58 us
    pallas_call x5 -> x6, Pallas kernels: 13.4 us -> 7.96 us  [call(): pl.pallas_call(kernel, name=name, out_shape=shapes if many else shapes[0]...]
    ppermute x1, starting transfers between devices: 5.23 us -> 2.48 us  [local(): turned = lax.ppermute(turned, EVERY, pairs)]
    ppermute x1, waiting for transfers between devices: 1.64 us -> 4.02 us  [local(): turned = lax.ppermute(turned, EVERY, pairs)]
    all_to_all x1, blocking collectives: 19.3 us -> 17.1 us  [local(): got3 = lax.all_to_all(block3, ('cont', 'core'), 0, 0, tiled=True)]
    all_to_all x1, blocking collectives: 19.8 us -> 21.7 us  [local(): got2 = lax.all_to_all(block2, 'cont', 0, 0, tiled=True)]
    ppermute x0 -> x1, starting transfers between devices: none -> 1.87 us  [local(): other1 = lax.ppermute(got1, 'core', [(0, 1), (1, 0)])]
    all_to_all x1, waiting for transfers between devices: 8.42 us -> 6.56 us  [local(): got1 = lax.all_to_all(block1, ('y', 'scen'), 0, 0, tiled=True)]
    all_to_all x1, starting transfers between devices: 8.6 us -> 7.59 us  [local(): got1 = lax.all_to_all(block1, ('y', 'scen'), 0, 0, tiled=True)]
  transfers between devices with their start and end apart: 2 -> 3, of which waited for: 2 -> 2; matrix products, arithmetic and copies ran while one was open for 6% -> 4% of each run, Pallas kernels for 0% -> 2%
where the time goes in v3:
time: 74.2 us; the launch traced here: 73.8 us
  blocking collectives  38.8 us (52%)
  starting transfers between devices  11.9 us (16%)
  waiting for transfers between devices  10.6 us (14%)
  Pallas kernels  7.96 us (11%)
  other arithmetic  2.58 us (3%)
  between operations  1.61 us (2%)
    all_to_all x1, blocking collectives, local(): got2 = lax.all_to_all(block2, 'cont', 0, 0, tiled=True)  21.7 us
    all_to_all x1, blocking collectives, local(): got3 = lax.all_to_all(block3, ('cont', 'core'), 0, 0, tiled=True)  17.1 us
    pallas_call x6, Pallas kernels, call(): pl.pallas_call(kernel, name=name, out_shape=shapes if many else shapes[0]...  7.96 us
    all_to_all x1, starting transfers between devices, local(): got1 = lax.all_to_all(block1, ('y', 'scen'), 0, 0, tiled=True)  7.59 us
    all_to_all x1, waiting for transfers between devices, local(): got1 = lax.all_to_all(block1, ('y', 'scen'), 0, 0, tiled=True)  6.56 us
    ppermute x1, waiting for transfers between devices, local(): turned = lax.ppermute(turned, EVERY, pairs)  4.02 us
    reduce_max x1, other arithmetic, local(): jnp.max(terms, axis=2)  2.54 us
    ppermute x1, starting transfers between devices, local(): turned = lax.ppermute(turned, EVERY, pairs)  2.48 us
  transfers between devices with their start and end apart: 3, of which 2 were waited for; matrix products, arithmetic and copies ran while one was open for 4% of the time, Pallas kernels for 2%

profile of v3, /device:TPU:1, one launch (start us, length us, event | category | flops | bytes accessed | tf_op | source)
XLA Modules:
  0.0 73.8 jit_solution(13075577961362558861)
XLA Ops:
  0.6 0.0 copy-start.3
  0.6 0.0 copy-start.2
  0.7 0.0 copy-start.4
  0.7 0.0 copy-start
  1.5 2.7 %prep.1 = bf16[16,96,128]{2,1,0:T(8,128)(2,1)} custom-call(s32[1]{0:T(128)S(6)} %copy.18.refs_0_, s32[4,128]{1,0:T(4,128)} %bitcast.12, s32[4,128]{1,0:T(4,128)} %bitcast.13, s32[4,128]{1,0:T(4,128)} %bitcast.14, bf16[128,512]{1,0:T(8,128)(2,1)} %refs_4_.1, f32[64,128]{1,0:T(8,128)} %bitcast.11, f32[64,512]{1,0:T(8,128)} %refs_6_.1, f32[1,128]{1,0:T(1,128)} %bitcast.9, ...), custom_call_target="tpu_custom_call" | custom-call | tf_op jit(solution)/shard_map/prep/pallas_call | solution.py:289
  4.2 7.6 %all-to-all-start = ((bf16[16,96,128]{2,1,0:T(8,128)(2,1)}), bf16[16,96,128]{2,1,0:T(8,128)(2,1)S(1)}, u32[]{:S(2)}, u32[]{:S(2)}) async-start(bf16[16,96,128]{2,1,0:T(8,128)(2,1)} %prep.1), calls=%async_computation | async-start | bytes 786432 | tf_op jit(solution)/shard_map/all_to_all | solution.py:329
  11.8 0.0 copy-done.2
  11.8 0.0 copy-done.3
  11.9 2.5 %multiply_reduce_fusion.1 = (f32[64,128]{1,0:T(8,128)S(1)}, f32[64,128]{1,0:T(8,128)S(1)}) fusion(f32[64,512]{1,0:T(8,128)S(1)} %copy-done.3, f32[128,512]{1,0:T(8,128)S(1)} %convert_element_type.3), kind=kLoop, calls=%fused_computation.1 | loop fusion | flops 12566528 | bytes 458752 | tf_op jit(solution)/shard_map/reduce_max | solution.py:335
  14.4 6.6 %all-to-all-done.got.own = bf16[16,96,128]{2,1,0:T(8,128)(2,1)S(1)} async-done(((bf16[16,96,128]{2,1,0:T(8,128)(2,1)}), bf16[16,96,128]{2,1,0:T(8,128)(2,1)S(1)}, u32[]{:S(2)}, u32[]{:S(2)}) %all-to-all-start) | async-done | bytes 393248 | tf_op jit(solution)/shard_map/all_to_all | solution.py:329
  21.0 1.9 %collective-permute-start = (bf16[16,96,128]{2,1,0:T(8,128)(2,1)S(1)}, bf16[16,96,128]{2,1,0:T(8,128)(2,1)S(1)}, u32[]{:S(2)}, u32[]{:S(2)}) collective-permute-start(bf16[16,96,128]{2,1,0:T(8,128)(2,1)S(1)} %all-to-all-done.got.own), channel_id=1, source_target_pairs={{0,4},{4,0},{1,5},{5,1},{2,6},{6,2},{3,7},{7,3},{8,12},{12,8},{9,1... | collective-permute-start | bytes 1179656 | tf_op jit(solution)/shard_map/ppermute | solution.py:330
  22.8 0.0 copy-done
  22.8 0.1 constant_dynamic-slice_fusion.1
  23.0 0.1 copy.16
  23.1 0.1 copy.17
  23.2 0.0 copy-done.4
  23.2 0.0 copy-start.1
  23.3 1.5 %first.1 = (f32[128,512]{1,0:T(8,128)S(1)}, f32[8,128]{1,0:T(8,128)S(1)}) custom-call(bf16[16,96,128]{2,1,0:T(8,128)(2,1)S(1)} %all-to-all-done.got.own), custom_call_target="tpu_custom_call" | custom-call | tf_op jit(solution)/shard_map/first/pallas_call | solution.py:289
  24.8 0.0 collective-permute-done.got.other
  24.8 2.0 %second.1 = bf16[8,160,128]{2,1,0:T(8,128)(2,1)S(1)} custom-call(bf16[16,96,128]{2,1,0:T(8,128)(2,1)S(1)} %collective-permute-done.got.other, f32[128,512]{1,0:T(8,128)S(1)} %get-tuple-element.9.part1, f32[8,128]{1,0:T(8,128)S(1)} %get-tuple-element.10.sums1, bf16[512,2048]{1,0:T(8,128)(2,1)S(1)} %copy-done, bf16[128,512]{1,0:T(8,128)(2,1)S(1)} %maximum_bitcast_fusion.own_t, ...), custom_call_target="tpu_custom_call" | custom-call | tf_op jit(solution)/shard_map/second/pallas_call | solution.py:289
  26.8 21.7 %all_to_all.15.got2 = bf16[8,160,128]{2,1,0:T(8,128)(2,1)S(1)} all-to-all(bf16[8,160,128]{2,1,0:T(8,128)(2,1)S(1)} %second.1), channel_id=1, replica_groups=mesh['cont'=8,'y'=4,'core'=2,'scen'=4] {'cont'}, dimensions={0} | all-to-all | bytes 655360 | tf_op jit(solution)/shard_map/all_to_all | solution.py:349
  48.6 0.0 copy-done.1
  48.6 0.6 combine.1
  49.2 2.5 %collective-permute-start.1 = (f32[128,128]{1,0:T(8,128)S(1)}, f32[128,128]{1,0:T(8,128)S(1)}, u32[]{:S(2)}, u32[]{:S(2)}) collective-permute-start(f32[128,128]{1,0:T(8,128)S(1)} %get-tuple-element.11), channel_id=1, source_target_pairs={{0,0},{1,1},{2,2},{3,3},{4,20},{5,21},{6,22},{7,23},{8,8},{9,9},{1... | collective-permute-start | bytes 196616 | tf_op jit(solution)/shard_map/ppermute | solution.py:368
  51.7 4.0 %collective-permute-done.1.turned = f32[128,128]{1,0:T(8,128)S(1)} collective-permute-done((f32[128,128]{1,0:T(8,128)S(1)}, f32[128,128]{1,0:T(8,128)S(1)}, u32[]{:S(2)}, u32[]{:S(2)}) %collective-permute-start.1) | collective-permute-done | bytes 65568 | tf_op jit(solution)/shard_map/ppermute | solution.py:368
  55.7 0.1 finish.1
  55.8 17.1 %all_to_all.16.got = s16[16,80,128]{2,1,0:T(8,128)(2,1)S(1)} all-to-all(s16[16,80,128]{2,1,0:T(8,128)(2,1)S(1)} %finish.1), channel_id=1, replica_groups=mesh['cont'=8,'y'=4,'core'=2,'scen'=4] {'cont','core'}, dimensions={0} | all-to-all | bytes 655360 | tf_op jit(solution)/shard_map/all_to_all | solution.py:375
  72.8 1.0 %place.1 = (f32[64,2048]{1,0:T(8,128)}, f32[64,128]{1,0:T(8,128)}) custom-call(s16[16,80,128]{2,1,0:T(8,128)(2,1)S(1)} %all_to_all.16.got), custom_call_target="tpu_custom_call" | custom-call | tf_op jit(solution)/shard_map/place/pallas_call | solution.py:289
  (3 shorter events, 0.0 us)
Async XLA Ops:
  0.6 11.2 %copy-start.3 = (f32[64,512]{1,0:T(8,128)S(1)}, f32[64,512]{1,0:T(8,128)}, u32[]{:S(2)}) copy-start(f32[64,512]{1,0:T(8,128)} %refs_6_.1) | copy-start | bytes 393220
  0.6 11.2 %copy-start.2 = (bf16[128,512]{1,0:T(8,128)(2,1)S(1)}, bf16[128,512]{1,0:T(8,128)(2,1)}, u32[]{:S(2)}) copy-start(bf16[128,512]{1,0:T(8,128)(2,1)} %refs_4_.1) | copy-start | bytes 393220
  0.7 22.6 %copy-start.4 = (f32[128,64]{0,1:T(8,128)S(1)}, f32[128,64]{0,1:T(8,128)}, u32[]{:S(2)}) copy-start(f32[128,64]{0,1:T(8,128)} %param.11) | copy-start | bytes 98308
  0.7 22.2 %copy-start = (bf16[512,2048]{1,0:T(8,128)(2,1)S(1)}, bf16[512,2048]{1,0:T(8,128)(2,1)}, u32[]{:S(2)}) copy-start(bf16[512,2048]{1,0:T(8,128)(2,1)} %out_rows.1) | copy-start | bytes 6291460
  4.2 16.8 %all-to-all-start = ((bf16[16,96,128]{2,1,0:T(8,128)(2,1)}), bf16[16,96,128]{2,1,0:T(8,128)(2,1)S(1)}, u32[]{:S(2)}, u32[]{:S(2)}) async-start(bf16[16,96,128]{2,1,0:T(8,128)(2,1)} %prep.1), calls=%async_computation | async-start | bytes 786432 | tf_op jit(solution)/shard_map/all_to_all | solution.py:329
  21.0 3.8 %collective-permute-start = (bf16[16,96,128]{2,1,0:T(8,128)(2,1)S(1)}, bf16[16,96,128]{2,1,0:T(8,128)(2,1)S(1)}, u32[]{:S(2)}, u32[]{:S(2)}) collective-permute-start(bf16[16,96,128]{2,1,0:T(8,128)(2,1)S(1)} %all-to-all-done.got.own), channel_id=1, source_target_pairs={{0,4},{4,0},{1,5},{5,1},{2,6},{6,2},{3,7},{7,3},{8,12},{12,8},{9,1... | collective-permute-start | bytes 1179656 | tf_op jit(solution)/shard_map/ppermute | solution.py:330
  23.2 25.3 %copy-start.1 = (f32[128]{0:T(128)S(1)}, f32[128]{0:T(128)}, u32[]{:S(2)}) copy-start(f32[128]{0:T(128)} %param.13) | copy-start | bytes 1540
  49.2 6.5 %collective-permute-start.1 = (f32[128,128]{1,0:T(8,128)S(1)}, f32[128,128]{1,0:T(8,128)S(1)}, u32[]{:S(2)}, u32[]{:S(2)}) collective-permute-start(f32[128,128]{1,0:T(8,128)S(1)} %get-tuple-element.11), channel_id=1, source_target_pairs={{0,0},{1,1},{2,2},{3,3},{4,20},{5,21},{6,22},{7,23},{8,8},{9,9},{1... | collective-permute-start | bytes 196616 | tf_op jit(solution)/shard_map/ppermute | solution.py:368

commit v4 on v3

--- a/solution.py
+++ b/solution.py
@@ -47,6 +47,29 @@
     rest = x - high.astype(F32)
     mid, low = split(rest)
     return high, mid, low
+
+
+ORDER1 = (16, False, 15)
+ORDER2 = (8, False, 4)
+ORDER3 = (8, False, 0, True)
+
+
+def spot(order, n, core):
+    size, reverse, other = order[:3]
+    bits = size.bit_length() - 1
+    if reverse:
+        n = sum(((n >> i) & 1) << (bits - 1 - i) for i in range(bits))
+    return n ^ (other * core) if other else n
+
+
+def spot3(c, core):
+    at = spot(ORDER3, c, core)
+    return core * 8 + at if ORDER3[3] else at * 2 + core
+
+
+def listed(order):
+    names = [sorted(range(order[0]), key=lambda n: spot(order, n, core)) for core in range(2)]
+    return names
 
 
 def place():
@@ -126,16 +149,19 @@
             part = jnp.concatenate(
                 [own[:, first : first + 64], own[:, first + 256 : first + 320]], axis=1
             )
-            out[yy * 4 + qq, M_OWN : M_OWN + 32, :] = part
+            out[spot(ORDER1, yy * 4 + qq, core), M_OWN : M_OWN + 32, :] = part
             for cc in range(2):
                 to_y = lax.bitwise_xor(jnp.int32(yy), 2 * cc + c // 4)
                 to = to_y * 4 + lax.bitwise_xor(jnp.int32(qq), c % 4)
                 lines = jnp.where(to < yy * 4 + qq, part[0:16].astype(F32), part[16:32].astype(F32))
                 first_row = M_TILE + 16 * cc
-                out[to, first_row : first_row + 16, :] = lines.astype(BF16)
-
-
-def half_product(got):
+                out[spot(ORDER1, to, core), first_row : first_row + 16, :] = lines.astype(BF16)
+
+
+def half_product(got, core):
+    def at(n):
+        return spot(ORDER1, n, core)
+
     def pieces(f, j):
         l, kl, low, up = f[j : j + 1], f[4 + j : 5 + j], f[8 + j : 9 + j], f[12 + j : 13 + j]
         is_l = iota((128, 128), 0).astype(F32) == l
@@ -147,30 +173,30 @@
 
     e_sum, d_rows, cores = jnp.zeros((8, 128), F32), [], []
     for yy in range(4):
-        tables = [got[yy * 4 + r, LIST : LIST + 32, :].astype(F32) for r in range(4)]
+        tables = [got[at(yy * 4 + r), LIST : LIST + 32, :].astype(F32) for r in range(4)]
         both = [pieces(f, j) for f in tables for j in range(4)]
-        core = dot(
+        blocks = dot(
             jnp.concatenate([p[0] for p in both], axis=1),
             jnp.concatenate([p[1] for p in both], axis=1),
             NT,
         )
-        cores.append(jnp.concatenate([core[:128], core[128:]], axis=1))
+        cores.append(jnp.concatenate([blocks[:128], blocks[128:]], axis=1))
         total = tables[0] + tables[1] + tables[2] + tables[3]
         e_sum = e_sum + total[16:24]
         d_rows.append(total[24:25] + total[25:26])
-    mon = jnp.concatenate([got[i, M_OWN : M_OWN + 32, :] for i in range(16)], axis=0)
+    mon = jnp.concatenate([got[at(i), M_OWN : M_OWN + 32, :] for i in range(16)], axis=0)
     high, low = split(jnp.concatenate(cores, axis=0))
     part = dot(mon, high, TN) + dot(mon, low, TN)
     return part, jnp.concatenate([e_sum[0:4] + e_sum[4:8], *d_rows], axis=0)
 
 
 def first_kernel(got, part, sums):
-    part[...], sums[...] = half_product(got)
+    part[...], sums[...] = half_product(got, lax.axis_index("core"))
 
 
 def second_kernel(got, part1, sums1, out_rows, own_t, screened, sent):
     c, y, core, q = place()
-    part, sums = half_product(got)
+    part, sums = half_product(got, 1 - core)
     e_sum = sums1[0:4, :] + sums[0:4]
     e_row = jnp.concatenate([e_sum[j : j + 1] for j in range(4)], axis=1)
     part = part1[...] + part + (0.5 * e_row) * own_t[...].astype(F32)
@@ -179,7 +205,7 @@
     d_rows = [p.astype(F32) for p in split(d_all)]
     for i in range(8):
         w_rows = [p.astype(F32) for p in split(screened[8 * i : 8 * i + 8, :])]
-        sent[i, TAIL2:BLOCK2, :] = jnp.concatenate([*w_rows, *d_rows], axis=0).astype(BF16)
+        sent[spot(ORDER2, i, core), TAIL2:BLOCK2, :] = jnp.concatenate([*w_rows, *d_rows], axis=0).astype(BF16)
     half = lax.bitwise_xor(y // 2, core)
     for yy in range(2):
         first = pl.multiple_of(half * 1024 + 512 * yy, 512)
@@ -187,7 +213,7 @@
         tile = (both[:128] + both[128:]).astype(BF16)
         for qq in range(4):
             to = lax.bitwise_xor(jnp.int32(yy), y % 2) * 4 + lax.bitwise_xor(jnp.int32(qq), q)
-            sent[to, 0:128, :] = jnp.concatenate(
+            sent[spot(ORDER2, to, core), 0:128, :] = jnp.concatenate(
                 [tile[:, 64 * qq : 64 * qq + 64], tile[:, 256 + 64 * qq : 320 + 64 * qq]], axis=1
             )
 
@@ -212,7 +238,8 @@
             for yy in range(4):
                 for r in range(4):
                     lines = pl.ds(pl.multiple_of(32 * r + 16 * h, 16), 16)
-                    mon = got[yy * 4 + r, pl.ds(pl.multiple_of(M_OWN + 16 * h, 16), 16), :]
+                    n = spot(ORDER1, yy * 4 + r, core if i == 0 else 1 - core)
+                    mon = got[n, pl.ds(pl.multiple_of(M_OWN + 16 * h, 16), 16), :]
                     scaled = mon.astype(F32) * d_ref[lines, 4 * i + yy : 4 * i + yy + 1]
                     lefts.append(jnp.concatenate(split(scaled), axis=1))
         return jnp.concatenate(lefts, axis=0)
@@ -228,7 +255,11 @@
     def _():
         both = 0.0
         for h in range(2):
-            rights = [g[i, M_OWN + 16 * h : M_OWN + 16 * h + 16, :] for g in (own, other) for i in range(16)]
+            rights = [
+                g[spot(ORDER1, n, k), M_OWN + 16 * h : M_OWN + 16 * h + 16, :]
+                for g, k in ((own, core), (other, 1 - core))
+                for n in range(16)
+            ]
             both = both + dot(side(h), jnp.concatenate(rights, axis=0), TN)
         write(both, 0.5)
 
@@ -238,7 +269,11 @@
         to_q = lax.bitwise_xor(q, c % 4)
         h = jnp.where(y * 4 + q < to_y * 4 + to_q, 0, 1)
         there = pl.ds(pl.multiple_of(M_TILE + 16 * core, 16), 16)
-        rights = [g[i, there, :] for g in (own, other) for i in range(16)]
+        rights = [
+            g[spot(ORDER1, n, k), there, :]
+            for g, k in ((own, core), (other, 1 - core))
+            for n in range(16)
+        ]
         write(dot(side(h), jnp.concatenate(rights, axis=0), TN), 1.0)
 
 
@@ -256,7 +291,7 @@
         rows = [code, worst_code, exp, worst_exp, jnp.zeros((BLOCK3 - 74, 128), F32)]
         block = jnp.concatenate(rows, axis=0).astype(jnp.int32).astype(I16)
         for i in range(8):
-            sent[2 * i + core, :, :] = block
+            sent[spot3(i, core), :, :] = block
 
 
 def decode(code, exponent):
@@ -271,13 +306,13 @@
             source_c = lax.bitwise_xor(jnp.int32(yy % 2), y % 2) * 4
             source_c = source_c + lax.bitwise_xor(jnp.int32(qq), q)
             source_core = lax.bitwise_xor(jnp.int32(yy // 2), y // 2)
-            block = got[source_c * 2 + source_core, :, :].astype(jnp.int32).astype(F32)
+            block = got[spot3(source_c, source_core), :, :].astype(jnp.int32).astype(F32)
             parts.append(decode(block[0:64], block[72:73]))
         schur[:, 512 * yy : 512 * yy + 512] = jnp.concatenate(
             [p[:, :64] for p in parts] + [p[:, 64:] for p in parts], axis=1
         )
     for i in range(8):
-        block = got[2 * i + core, 64:80, :].astype(jnp.int32).astype(F32)
+        block = got[spot3(i, core), 64:80, :].astype(jnp.int32).astype(F32)
         worst[8 * i : 8 * i + 8, :] = decode(block[0:8], block[9:10])
 
 
@@ -326,7 +361,13 @@
     block1 = call(
         prep_kernel, "prep", [((16, BLOCK1, 128), BF16)], *inputs, scratch=scratch, space=pl.ANY, vmem_mib=60
     )
-    got1 = lax.all_to_all(block1, ("y", "scen"), 0, 0, tiled=True)
+    groups1 = [
+        [((n // 4) * 2 + core) * 4 + n % 4 for n in names]
+        for core, names in enumerate(listed(ORDER1))
+    ]
+    got1 = lax.all_to_all(
+        block1, ("y", "core", "scen"), 0, 0, axis_index_groups=groups1, tiled=True
+    )
     other1 = lax.ppermute(got1, "core", [(0, 1), (1, 0)])
 
     wide = lodf.astype(F32)
@@ -346,7 +387,10 @@
         [((8, BLOCK2, 128), BF16)],
         other1, part, sums, ptdf_out, own_t, screened,
     )
-    got2 = lax.all_to_all(block2, "cont", 0, 0, tiled=True)
+    groups2 = [[c * 2 + core for c in names] for core, names in enumerate(listed(ORDER2))]
+    got2 = lax.all_to_all(
+        block2, ("cont", "core"), 0, 0, axis_index_groups=groups2, tiled=True
+    )
     turned, direct, worst_part = call(
         combine_kernel,
         "combine",
@@ -372,7 +416,10 @@
         [((16, BLOCK3, 128), I16)],
         turned, direct, worst_part,
     )
-    got3 = lax.all_to_all(block3, ("cont", "core"), 0, 0, tiled=True)
+    group3 = sorted(range(16), key=lambda n: spot3(n // 2, n % 2))
+    got3 = lax.all_to_all(
+        block3, ("cont", "core"), 0, 0, axis_index_groups=[group3], tiled=True
+    )
     schur, worst_t = call(
         place_kernel, "place", [((64, 2048), F32), ((64, 128), F32)], got3
     )

time: 74.2 us -> 71 us (0.957)
  waiting for transfers between devices: 10.6 us -> 6.63 us
  starting transfers between devices: 11.9 us -> 15.2 us
  blocking collectives: 38.8 us -> 36.2 us
    all_to_all x1, waiting for transfers between devices: 6.56 us -> 2.65 us  [local(): lax.all_to_all(block1, ('y', 'core', 'scen'), 0, 0, axis_index_groups=gro...]
    all_to_all x2, blocking collectives: 38.8 us -> 36.2 us  [the longest x1 18.5 us: local(): lax.all_to_all(block3, ('cont', 'core'), 0, 0, axis_index_groups=[group3]...]
    ppermute x1, starting transfers between devices: 1.87 us -> 3.5 us  [local(): other1 = lax.ppermute(got1, 'core', [(0, 1), (1, 0)])]
    all_to_all x1, starting transfers between devices: 7.59 us -> 9.21 us  [local(): lax.all_to_all(block1, ('y', 'core', 'scen'), 0, 0, axis_index_groups=gro...]
where the time goes in v4:
time: 71 us; the launch traced here: 70.6 us
  blocking collectives  36.2 us (51%)
  starting transfers between devices  15.2 us (21%)
  Pallas kernels  7.99 us (11%)
  waiting for transfers between devices  6.63 us (9%)
  other arithmetic  2.58 us (4%)
  between operations  1.6 us (2%)
    all_to_all x1, blocking collectives, local(): lax.all_to_all(block3, ('cont', 'core'), 0, 0, axis_index_groups=[group3]...  18.5 us
    all_to_all x1, blocking collectives, local(): lax.all_to_all(block2, ('cont', 'core'), 0, 0, axis_index_groups=groups2,...  17.6 us
    all_to_all x1, starting transfers between devices, local(): lax.all_to_all(block1, ('y', 'core', 'scen'), 0, 0, axis_index_groups=gro...  9.21 us
    pallas_call x6, Pallas kernels, call(): pl.pallas_call(kernel, name=name, out_shape=shapes if many else shapes[0]...  7.99 us
    ppermute x1, waiting for transfers between devices, local(): turned = lax.ppermute(turned, EVERY, pairs)  3.98 us
    ppermute x1, starting transfers between devices, local(): other1 = lax.ppermute(got1, 'core', [(0, 1), (1, 0)])  3.5 us
    all_to_all x1, waiting for transfers between devices, local(): lax.all_to_all(block1, ('y', 'core', 'scen'), 0, 0, axis_index_groups=gro...  2.65 us
    reduce_max x1, other arithmetic, local(): jnp.max(terms, axis=2)  2.54 us
  transfers between devices with their start and end apart: 3, of which 2 were waited for; matrix products, arithmetic and copies ran while one was open for 4% of the time, Pallas kernels for 2%

profile of v4, /device:TPU:1, one launch (start us, length us, event | category | flops | bytes accessed | tf_op | source)
XLA Modules:
  0.0 70.6 jit_solution(15411359038240919681)
XLA Ops:
  0.6 0.0 copy-start.3
  0.6 0.0 copy-start.2
  0.7 0.0 copy-start.4
  0.7 0.0 copy-start
  1.5 2.7 %prep.1 = bf16[16,96,128]{2,1,0:T(8,128)(2,1)} custom-call(s32[1]{0:T(128)S(6)} %copy.18.refs_0_, s32[4,128]{1,0:T(4,128)} %bitcast.12, s32[4,128]{1,0:T(4,128)} %bitcast.13, s32[4,128]{1,0:T(4,128)} %bitcast.14, bf16[128,512]{1,0:T(8,128)(2,1)} %refs_4_.1, f32[64,128]{1,0:T(8,128)} %bitcast.11, f32[64,512]{1,0:T(8,128)} %refs_6_.1, f32[1,128]{1,0:T(1,128)} %bitcast.9, ...), custom_call_target="tpu_custom_call" | custom-call | tf_op jit(solution)/shard_map/prep/pallas_call | solution.py:324
  4.2 9.2 %all-to-all-start = ((bf16[16,96,128]{2,1,0:T(8,128)(2,1)}), bf16[16,96,128]{2,1,0:T(8,128)(2,1)S(1)}, u32[]{:S(2)}, u32[]{:S(2)}) async-start(bf16[16,96,128]{2,1,0:T(8,128)(2,1)} %prep.1), calls=%async_computation | async-start | bytes 786432 | tf_op jit(solution)/shard_map/all_to_all | solution.py:368
  13.4 0.0 copy-done.2
  13.4 0.0 copy-done.3
  13.5 2.5 %multiply_reduce_fusion.1 = (f32[64,128]{1,0:T(8,128)S(1)}, f32[64,128]{1,0:T(8,128)S(1)}) fusion(f32[64,512]{1,0:T(8,128)S(1)} %copy-done.3, f32[128,512]{1,0:T(8,128)S(1)} %convert_element_type.3), kind=kLoop, calls=%fused_computation.1 | loop fusion | flops 12566528 | bytes 458752 | tf_op jit(solution)/shard_map/reduce_max | solution.py:376
  16.0 2.7 %all-to-all-done.got.own = bf16[16,96,128]{2,1,0:T(8,128)(2,1)S(1)} async-done(((bf16[16,96,128]{2,1,0:T(8,128)(2,1)}), bf16[16,96,128]{2,1,0:T(8,128)(2,1)S(1)}, u32[]{:S(2)}, u32[]{:S(2)}) %all-to-all-start) | async-done | bytes 393248 | tf_op jit(solution)/shard_map/all_to_all | solution.py:368
  18.7 3.5 %collective-permute-start = (bf16[16,96,128]{2,1,0:T(8,128)(2,1)S(1)}, bf16[16,96,128]{2,1,0:T(8,128)(2,1)S(1)}, u32[]{:S(2)}, u32[]{:S(2)}) collective-permute-start(bf16[16,96,128]{2,1,0:T(8,128)(2,1)S(1)} %all-to-all-done.got.own), channel_id=1, source_target_pairs={{0,4},{4,0},{1,5},{5,1},{2,6},{6,2},{3,7},{7,3},{8,12},{12,8},{9,1... | collective-permute-start | bytes 1179656 | tf_op jit(solution)/shard_map/ppermute | solution.py:371
  22.1 0.0 copy-done
  22.2 0.1 constant_dynamic-slice_fusion.1
  22.3 0.1 copy.16
  22.4 0.1 copy.17
  22.5 0.0 copy-done.4
  22.6 0.0 copy-start.1
  22.6 1.6 %first.1 = (f32[128,512]{1,0:T(8,128)S(1)}, f32[8,128]{1,0:T(8,128)S(1)}) custom-call(bf16[16,96,128]{2,1,0:T(8,128)(2,1)S(1)} %all-to-all-done.got.own), custom_call_target="tpu_custom_call" | custom-call | tf_op jit(solution)/shard_map/first/pallas_call | solution.py:324
  24.1 0.0 collective-permute-done.got.other
  24.2 2.0 %second.1 = bf16[8,160,128]{2,1,0:T(8,128)(2,1)S(1)} custom-call(bf16[16,96,128]{2,1,0:T(8,128)(2,1)S(1)} %collective-permute-done.got.other, f32[128,512]{1,0:T(8,128)S(1)} %get-tuple-element.9.part1, f32[8,128]{1,0:T(8,128)S(1)} %get-tuple-element.10.sums1, bf16[512,2048]{1,0:T(8,128)(2,1)S(1)} %copy-done, bf16[128,512]{1,0:T(8,128)(2,1)S(1)} %maximum_bitcast_fusion.own_t, ...), custom_call_target="tpu_custom_call" | custom-call | tf_op jit(solution)/shard_map/second/pallas_call | solution.py:324
  26.2 17.6 %all_to_all.15.got2 = bf16[8,160,128]{2,1,0:T(8,128)(2,1)S(1)} all-to-all(bf16[8,160,128]{2,1,0:T(8,128)(2,1)S(1)} %second.1), channel_id=1, replica_groups={{0,32,64,96,128,160,192,224},{132,164,196,228,4,36,68,100},{1,33,65,97,..., dimensions={0} | all-to-all | bytes 655360 | tf_op jit(solution)/shard_map/all_to_all | solution.py:391
  43.8 0.0 copy-done.1
  43.8 0.6 combine.1
  44.4 2.5 %collective-permute-start.1 = (f32[128,128]{1,0:T(8,128)S(1)}, f32[128,128]{1,0:T(8,128)S(1)}, u32[]{:S(2)}, u32[]{:S(2)}) collective-permute-start(f32[128,128]{1,0:T(8,128)S(1)} %get-tuple-element.11), channel_id=1, source_target_pairs={{0,0},{1,1},{2,2},{3,3},{4,20},{5,21},{6,22},{7,23},{8,8},{9,9},{1... | collective-permute-start | bytes 196616 | tf_op jit(solution)/shard_map/ppermute | solution.py:412
  47.0 4.0 %collective-permute-done.1.turned = f32[128,128]{1,0:T(8,128)S(1)} collective-permute-done((f32[128,128]{1,0:T(8,128)S(1)}, f32[128,128]{1,0:T(8,128)S(1)}, u32[]{:S(2)}, u32[]{:S(2)}) %collective-permute-start.1) | collective-permute-done | bytes 65568 | tf_op jit(solution)/shard_map/ppermute | solution.py:412
  50.9 0.1 finish.1
  51.0 18.5 %all_to_all.16.got = s16[16,80,128]{2,1,0:T(8,128)(2,1)S(1)} all-to-all(s16[16,80,128]{2,1,0:T(8,128)(2,1)S(1)} %finish.1), channel_id=1, replica_groups={{0,32,64,96,128,160,192,224,4,36,68,100,132,164,196,228},{1,33,65,97,12..., dimensions={0} | all-to-all | bytes 655360 | tf_op jit(solution)/shard_map/all_to_all | solution.py:420
  69.6 1.0 %place.1 = (f32[64,2048]{1,0:T(8,128)}, f32[64,128]{1,0:T(8,128)}) custom-call(s16[16,80,128]{2,1,0:T(8,128)(2,1)S(1)} %all_to_all.16.got), custom_call_target="tpu_custom_call" | custom-call | tf_op jit(solution)/shard_map/place/pallas_call | solution.py:324
  (3 shorter events, 0.0 us)
Async XLA Ops:
  0.6 12.8 %copy-start.3 = (f32[64,512]{1,0:T(8,128)S(1)}, f32[64,512]{1,0:T(8,128)}, u32[]{:S(2)}) copy-start(f32[64,512]{1,0:T(8,128)} %refs_6_.1) | copy-start | bytes 393220
  0.6 12.8 %copy-start.2 = (bf16[128,512]{1,0:T(8,128)(2,1)S(1)}, bf16[128,512]{1,0:T(8,128)(2,1)}, u32[]{:S(2)}) copy-start(bf16[128,512]{1,0:T(8,128)(2,1)} %refs_4_.1) | copy-start | bytes 393220
  0.7 21.9 %copy-start.4 = (f32[128,64]{0,1:T(8,128)S(1)}, f32[128,64]{0,1:T(8,128)}, u32[]{:S(2)}) copy-start(f32[128,64]{0,1:T(8,128)} %param.11) | copy-start | bytes 98308
  0.7 21.5 %copy-start = (bf16[512,2048]{1,0:T(8,128)(2,1)S(1)}, bf16[512,2048]{1,0:T(8,128)(2,1)}, u32[]{:S(2)}) copy-start(bf16[512,2048]{1,0:T(8,128)(2,1)} %out_rows.1) | copy-start | bytes 6291460
  4.2 14.5 %all-to-all-start = ((bf16[16,96,128]{2,1,0:T(8,128)(2,1)}), bf16[16,96,128]{2,1,0:T(8,128)(2,1)S(1)}, u32[]{:S(2)}, u32[]{:S(2)}) async-start(bf16[16,96,128]{2,1,0:T(8,128)(2,1)} %prep.1), calls=%async_computation | async-start | bytes 786432 | tf_op jit(solution)/shard_map/all_to_all | solution.py:368
  18.7 5.5 %collective-permute-start = (bf16[16,96,128]{2,1,0:T(8,128)(2,1)S(1)}, bf16[16,96,128]{2,1,0:T(8,128)(2,1)S(1)}, u32[]{:S(2)}, u32[]{:S(2)}) collective-permute-start(bf16[16,96,128]{2,1,0:T(8,128)(2,1)S(1)} %all-to-all-done.got.own), channel_id=1, source_target_pairs={{0,4},{4,0},{1,5},{5,1},{2,6},{6,2},{3,7},{7,3},{8,12},{12,8},{9,1... | collective-permute-start | bytes 1179656 | tf_op jit(solution)/shard_map/ppermute | solution.py:371
  22.6 21.3 %copy-start.1 = (f32[128]{0:T(128)S(1)}, f32[128]{0:T(128)}, u32[]{:S(2)}) copy-start(f32[128]{0:T(128)} %param.13) | copy-start | bytes 1540
  44.4 6.5 %collective-permute-start.1 = (f32[128,128]{1,0:T(8,128)S(1)}, f32[128,128]{1,0:T(8,128)S(1)}, u32[]{:S(2)}, u32[]{:S(2)}) collective-permute-start(f32[128,128]{1,0:T(8,128)S(1)} %get-tuple-element.11), channel_id=1, source_target_pairs={{0,0},{1,1},{2,2},{3,3},{4,20},{5,21},{6,22},{7,23},{8,8},{9,9},{1... | collective-permute-start | bytes 196616 | tf_op jit(solution)/shard_map/ppermute | solution.py:412

commit v5 on v4

--- a/solution.py
+++ b/solution.py
@@ -218,6 +218,16 @@
             )
 
 
+def encode(x):
+    top = jnp.maximum(jnp.max(jnp.abs(x), axis=0, keepdims=True), 1e-30)
+    exponent = jnp.floor(jnp.log2(top) + 1.001) - 15.0
+    return jnp.floor(x * jnp.exp2(-exponent) + 0.5), exponent
+
+
+def decode(code, exponent):
+    return code * jnp.exp2(exponent)
+
+
 def combine_kernel(got2, own, other, limits, turned, direct, worst, d_ref):
     c, y, core, q = place()
     a = got2[0, 0:128, :].astype(F32)
@@ -247,7 +257,9 @@
     def write(both, factor):
         total = a + factor * (both[:128] + both[128:])
         direct[...] = total
-        turned[...] = total.T
+        code, exp = encode(total.T)
+        rows = [code, exp, jnp.zeros((15, 128), F32)]
+        turned[...] = jnp.concatenate(rows, axis=0).astype(jnp.int32).astype(I16)
 
     alone = (c == 0) & (core == 0)
 
@@ -277,14 +289,9 @@
         write(dot(side(h), jnp.concatenate(rights, axis=0), TN), 1.0)
 
 
-def encode(x):
-    top = jnp.maximum(jnp.max(jnp.abs(x), axis=0, keepdims=True), 1e-30)
-    exponent = jnp.floor(jnp.log2(top) + 1.001) - 15.0
-    return jnp.floor(x * jnp.exp2(-exponent) + 0.5), exponent
-
-
 def finish_kernel(scale, turned, direct, worst, sent):
-    tile = (direct[...] + turned[...]) * scale
+    other = turned[...].astype(jnp.int32).astype(F32)
+    tile = (direct[...] + decode(other[:128], other[128:129])) * scale
     worst_code, worst_exp = encode(worst[...])
     for core in range(2):
         code, exp = encode(tile[64 * core : 64 * core + 64, :])
@@ -292,10 +299,6 @@
         block = jnp.concatenate(rows, axis=0).astype(jnp.int32).astype(I16)
         for i in range(8):
             sent[spot3(i, core), :, :] = block
-
-
-def decode(code, exponent):
-    return code * jnp.exp2(exponent)
 
 
 def place_kernel(got, schur, worst):
@@ -368,7 +371,6 @@
     got1 = lax.all_to_all(
         block1, ("y", "core", "scen"), 0, 0, axis_index_groups=groups1, tiled=True
     )
-    other1 = lax.ppermute(got1, "core", [(0, 1), (1, 0)])
 
     wide = lodf.astype(F32)
     terms = wide[None, :, :] * out_flow[:, None, :]
@@ -380,6 +382,8 @@
         [lax.dynamic_slice_in_dim(ptdf_out, first + 256 * i, 64, 1) for i in range(2)], axis=1
     ).T
 
+    got1, own_t, screened = lax.optimization_barrier((got1, own_t, screened))
+    other1 = lax.ppermute(got1, "core", [(0, 1), (1, 0)])
     part, sums = call(first_kernel, "first", [((128, 512), F32), ((8, 128), F32)], got1)
     block2 = call(
         second_kernel,
@@ -394,7 +398,7 @@
     turned, direct, worst_part = call(
         combine_kernel,
         "combine",
-        [((128, 128), F32), ((128, 128), F32), ((8, 128), F32)],
+        [((144, 128), I16), ((128, 128), F32), ((8, 128), F32)],
         got2, got1, other1, ratings,
         scratch=[pltpu.VMEM((128, 8), F32)],
     )

time: 71 us -> 70.3 us (level)
  waiting for transfers between devices: 6.63 us -> 5.92 us
where the time goes in v5:
time: 70.3 us; the launch traced here: 69.8 us
  blocking collectives  36.1 us (51%)
  starting transfers between devices  15.2 us (22%)
  Pallas kernels  8.03 us (11%)
  waiting for transfers between devices  5.92 us (8%)
  other arithmetic  2.58 us (4%)
  between operations  1.61 us (2%)
    all_to_all x1, blocking collectives, local(): lax.all_to_all(block3, ('cont', 'core'), 0, 0, axis_index_groups=[group3]...  18.8 us
    all_to_all x1, blocking collectives, local(): lax.all_to_all(block2, ('cont', 'core'), 0, 0, axis_index_groups=groups2,...  17.4 us
    all_to_all x1, starting transfers between devices, local(): lax.all_to_all(block1, ('y', 'core', 'scen'), 0, 0, axis_index_groups=gro...  9.21 us
    pallas_call x6, Pallas kernels, call(): pl.pallas_call(kernel, name=name, out_shape=shapes if many else shapes[0]...  8.03 us
    ppermute x1, waiting for transfers between devices, local(): turned = lax.ppermute(turned, EVERY, pairs)  3.7 us
    ppermute x1, starting transfers between devices, local(): other1 = lax.ppermute(got1, 'core', [(0, 1), (1, 0)])  3.5 us
    reduce_max x1, other arithmetic, local(): jnp.max(terms, axis=2)  2.54 us
    ppermute x1, starting transfers between devices, local(): turned = lax.ppermute(turned, EVERY, pairs)  2.5 us
  transfers between devices with their start and end apart: 3, of which 2 were waited for; matrix products, arithmetic and copies ran while one was open for 4% of the time, Pallas kernels for 2%

profile of v5, /device:TPU:1, one launch (start us, length us, event | category | flops | bytes accessed | tf_op | source)
XLA Modules:
  0.0 69.8 jit_solution(6596145031395449003)
XLA Ops:
  0.6 0.0 copy-start.3
  0.6 0.0 copy-start.2
  0.7 0.0 copy-start.4
  0.7 0.0 copy-start
  1.5 2.7 %prep.1 = bf16[16,96,128]{2,1,0:T(8,128)(2,1)} custom-call(s32[1]{0:T(128)S(6)} %copy.18.refs_0_, s32[4,128]{1,0:T(4,128)} %bitcast.12, s32[4,128]{1,0:T(4,128)} %bitcast.13, s32[4,128]{1,0:T(4,128)} %bitcast.14, bf16[128,512]{1,0:T(8,128)(2,1)} %refs_4_.1, f32[64,128]{1,0:T(8,128)} %bitcast.11, f32[64,512]{1,0:T(8,128)} %refs_6_.1, f32[1,128]{1,0:T(1,128)} %bitcast.9, ...), custom_call_target="tpu_custom_call" | custom-call | tf_op jit(solution)/shard_map/prep/pallas_call | solution.py:327
  4.2 9.2 %all-to-all-start = ((bf16[16,96,128]{2,1,0:T(8,128)(2,1)}), bf16[16,96,128]{2,1,0:T(8,128)(2,1)S(1)}, u32[]{:S(2)}, u32[]{:S(2)}) async-start(bf16[16,96,128]{2,1,0:T(8,128)(2,1)} %prep.1), calls=%async_computation | async-start | bytes 786432 | tf_op jit(solution)/shard_map/all_to_all | solution.py:371
  13.4 0.0 copy-done.2
  13.4 0.0 copy-done.3
  13.5 2.5 %multiply_reduce_fusion.1 = (f32[64,128]{1,0:T(8,128)S(1)}, f32[64,128]{1,0:T(8,128)S(1)}) fusion(f32[64,512]{1,0:T(8,128)S(1)} %copy-done.3, f32[128,512]{1,0:T(8,128)S(1)} %convert_element_type.3), kind=kLoop, calls=%fused_computation.1 | loop fusion | flops 12566528 | bytes 458752 | tf_op jit(solution)/shard_map/reduce_max | solution.py:378
  16.0 0.0 copy-done
  16.0 0.2 constant_dynamic-slice_fusion.1
  16.2 0.1 copy.16
  16.3 0.1 copy.17
  16.4 0.0 copy-done.4
  16.4 0.0 copy-start.1
  16.4 2.2 %all-to-all-done.got.own = bf16[16,96,128]{2,1,0:T(8,128)(2,1)S(1)} async-done(((bf16[16,96,128]{2,1,0:T(8,128)(2,1)}), bf16[16,96,128]{2,1,0:T(8,128)(2,1)S(1)}, u32[]{:S(2)}, u32[]{:S(2)}) %all-to-all-start) | async-done | bytes 393248 | tf_op jit(solution)/shard_map/all_to_all | solution.py:371
  18.7 3.5 %collective-permute-start = (bf16[16,96,128]{2,1,0:T(8,128)(2,1)S(1)}, bf16[16,96,128]{2,1,0:T(8,128)(2,1)S(1)}, u32[]{:S(2)}, u32[]{:S(2)}) collective-permute-start(bf16[16,96,128]{2,1,0:T(8,128)(2,1)S(1)} %all-to-all-done.got.own), channel_id=1, source_target_pairs={{0,4},{4,0},{1,5},{5,1},{2,6},{6,2},{3,7},{7,3},{8,12},{12,8},{9,1... | collective-permute-start | bytes 1179656 | tf_op jit(solution)/shard_map/ppermute | solution.py:386
  22.1 1.6 %first.1 = (f32[128,512]{1,0:T(8,128)S(1)}, f32[8,128]{1,0:T(8,128)S(1)}) custom-call(bf16[16,96,128]{2,1,0:T(8,128)(2,1)S(1)} %all-to-all-done.got.own), custom_call_target="tpu_custom_call" | custom-call | tf_op jit(solution)/shard_map/first/pallas_call | solution.py:327
  23.7 0.0 collective-permute-done.got.other
  23.7 2.0 %second.1 = bf16[8,160,128]{2,1,0:T(8,128)(2,1)S(1)} custom-call(bf16[16,96,128]{2,1,0:T(8,128)(2,1)S(1)} %collective-permute-done.got.other, f32[128,512]{1,0:T(8,128)S(1)} %get-tuple-element.13.part1, f32[8,128]{1,0:T(8,128)S(1)} %get-tuple-element.14.sums1, bf16[512,2048]{1,0:T(8,128)(2,1)S(1)} %copy-done, ...), custom_call_target="tpu_custom_call" | custom-call | tf_op jit(solution)/shard_map/second/pallas_call | solution.py:327
  25.7 17.4 %all_to_all.15.got2 = bf16[8,160,128]{2,1,0:T(8,128)(2,1)S(1)} all-to-all(bf16[8,160,128]{2,1,0:T(8,128)(2,1)S(1)} %second.1), channel_id=1, replica_groups={{0,32,64,96,128,160,192,224},{132,164,196,228,4,36,68,100},{1,33,65,97,..., dimensions={0} | all-to-all | bytes 655360 | tf_op jit(solution)/shard_map/all_to_all | solution.py:395
  43.1 0.0 copy-done.1
  43.1 0.7 combine.1
  43.8 2.5 %collective-permute-start.1 = (s16[144,128]{1,0:T(8,128)(2,1)S(1)}, s16[144,128]{1,0:T(8,128)(2,1)S(1)}, u32[]{:S(2)}, u32[]{:S(2)}) collective-permute-start(s16[144,128]{1,0:T(8,128)(2,1)S(1)} %get-tuple-element.17), channel_id=1, source_target_pairs={{0,0},{1,1},{2,2},{3,3},{4,20},{5,21},{6,22},{7,23},{8,8},{9,9},{1... | collective-permute-start | bytes 110600 | tf_op jit(solution)/shard_map/ppermute | solution.py:416
  46.3 3.7 %collective-permute-done.1.turned = s16[144,128]{1,0:T(8,128)(2,1)S(1)} collective-permute-done((s16[144,128]{1,0:T(8,128)(2,1)S(1)}, s16[144,128]{1,0:T(8,128)(2,1)S(1)}, u32[]{:S(2)}, u32[]{:S(2)}) %collective-permute-start.1) | collective-permute-done | bytes 36896 | tf_op jit(solution)/shard_map/ppermute | solution.py:416
  50.0 0.1 finish.1
  50.0 18.8 %all_to_all.16.got = s16[16,80,128]{2,1,0:T(8,128)(2,1)S(1)} all-to-all(s16[16,80,128]{2,1,0:T(8,128)(2,1)S(1)} %finish.1), channel_id=1, replica_groups={{0,32,64,96,128,160,192,224,4,36,68,100,132,164,196,228},{1,33,65,97,12..., dimensions={0} | all-to-all | bytes 655360 | tf_op jit(solution)/shard_map/all_to_all | solution.py:424
  68.8 1.0 %place.1 = (f32[64,2048]{1,0:T(8,128)}, f32[64,128]{1,0:T(8,128)}) custom-call(s16[16,80,128]{2,1,0:T(8,128)(2,1)S(1)} %all_to_all.16.got), custom_call_target="tpu_custom_call" | custom-call | tf_op jit(solution)/shard_map/place/pallas_call | solution.py:327
  (3 shorter events, 0.0 us)
Async XLA Ops:
  0.6 12.8 %copy-start.3 = (f32[64,512]{1,0:T(8,128)S(1)}, f32[64,512]{1,0:T(8,128)}, u32[]{:S(2)}) copy-start(f32[64,512]{1,0:T(8,128)} %refs_6_.1) | copy-start | bytes 393220
  0.6 12.8 %copy-start.2 = (bf16[128,512]{1,0:T(8,128)(2,1)S(1)}, bf16[128,512]{1,0:T(8,128)(2,1)}, u32[]{:S(2)}) copy-start(bf16[128,512]{1,0:T(8,128)(2,1)} %refs_4_.1) | copy-start | bytes 393220
  0.7 15.7 %copy-start.4 = (f32[128,64]{0,1:T(8,128)S(1)}, f32[128,64]{0,1:T(8,128)}, u32[]{:S(2)}) copy-start(f32[128,64]{0,1:T(8,128)} %param.11) | copy-start | bytes 98308
  0.7 15.3 %copy-start = (bf16[512,2048]{1,0:T(8,128)(2,1)S(1)}, bf16[512,2048]{1,0:T(8,128)(2,1)}, u32[]{:S(2)}) copy-start(bf16[512,2048]{1,0:T(8,128)(2,1)} %out_rows.1) | copy-start | bytes 6291460
  4.2 14.5 %all-to-all-start = ((bf16[16,96,128]{2,1,0:T(8,128)(2,1)}), bf16[16,96,128]{2,1,0:T(8,128)(2,1)S(1)}, u32[]{:S(2)}, u32[]{:S(2)}) async-start(bf16[16,96,128]{2,1,0:T(8,128)(2,1)} %prep.1), calls=%async_computation | async-start | bytes 786432 | tf_op jit(solution)/shard_map/all_to_all | solution.py:371
  16.4 26.7 %copy-start.1 = (f32[128]{0:T(128)S(1)}, f32[128]{0:T(128)}, u32[]{:S(2)}) copy-start(f32[128]{0:T(128)} %param.13) | copy-start | bytes 1540
  18.7 5.1 %collective-permute-start = (bf16[16,96,128]{2,1,0:T(8,128)(2,1)S(1)}, bf16[16,96,128]{2,1,0:T(8,128)(2,1)S(1)}, u32[]{:S(2)}, u32[]{:S(2)}) collective-permute-start(bf16[16,96,128]{2,1,0:T(8,128)(2,1)S(1)} %all-to-all-done.got.own), channel_id=1, source_target_pairs={{0,4},{4,0},{1,5},{5,1},{2,6},{6,2},{3,7},{7,3},{8,12},{12,8},{9,1... | collective-permute-start | bytes 1179656 | tf_op jit(solution)/shard_map/ppermute | solution.py:386
  43.8 6.2 %collective-permute-start.1 = (s16[144,128]{1,0:T(8,128)(2,1)S(1)}, s16[144,128]{1,0:T(8,128)(2,1)S(1)}, u32[]{:S(2)}, u32[]{:S(2)}) collective-permute-start(s16[144,128]{1,0:T(8,128)(2,1)S(1)} %get-tuple-element.17), channel_id=1, source_target_pairs={{0,0},{1,1},{2,2},{3,3},{4,20},{5,21},{6,22},{7,23},{8,8},{9,9},{1... | collective-permute-start | bytes 110600 | tf_op jit(solution)/shard_map/ppermute | solution.py:416

commit v6 on v5

--- a/solution.py
+++ b/solution.py
@@ -78,17 +78,37 @@
 
 def prep_kernel(*refs):
     hbm, out, local, sems = refs[:9], refs[9], refs[10:19], refs[19]
+    block, out_sems = refs[20], refs[21]
     c, y, core, q = place()
     lines_here = pl.ds(pl.multiple_of(q * 32, 32), 32)
     copies = []
     for i, (source, target) in enumerate(zip(hbm, local)):
         source = source.at[lines_here, :] if i == 8 else source
         copies.append(pltpu.make_async_copy(source, target, sems.at[i]))
-    for copy in copies:
+    for copy in copies[8:] + copies[:8]:
         copy.start()
-    for copy in copies:
+    used, k4, l4, s4, lodf, flow, out_flow, limits, own_ref = local
+    copies[8].wait()
+    own = own_ref[...]
+    for yy in range(4):
+        for qq in range(4):
+            first = 512 * yy + 64 * qq
+            part = jnp.concatenate(
+                [own[:, first : first + 64], own[:, first + 256 : first + 320]], axis=1
+            )
+            block[spot(ORDER1, yy * 4 + qq, core), M_OWN : M_OWN + 32, :] = part
+            for cc in range(2):
+                to_y = lax.bitwise_xor(jnp.int32(yy), 2 * cc + c // 4)
+                to = to_y * 4 + lax.bitwise_xor(jnp.int32(qq), c % 4)
+                lines = jnp.where(to < yy * 4 + qq, part[0:16].astype(F32), part[16:32].astype(F32))
+                first_row = M_TILE + 16 * cc
+                block[spot(ORDER1, to, core), first_row : first_row + 16, :] = lines.astype(BF16)
+    mon_out = pltpu.make_async_copy(
+        block.at[:, 0:LIST, :], out.at[:, 0:LIST, :], out_sems.at[0]
+    )
+    mon_out.start()
+    for copy in copies[:8]:
         copy.wait()
-    used, k4, l4, s4, lodf, flow, out_flow, limits, own_ref = local
     n = 512
 
     def row(ref):
@@ -140,22 +160,13 @@
     rows += [jnp.zeros((32 - len(rows), 128), F32)]
     table = jnp.concatenate(rows, axis=0).astype(BF16)
     for b in range(16):
-        out[b, LIST : LIST + 32, :] = table
-
-    own = own_ref[...]
-    for yy in range(4):
-        for qq in range(4):
-            first = 512 * yy + 64 * qq
-            part = jnp.concatenate(
-                [own[:, first : first + 64], own[:, first + 256 : first + 320]], axis=1
-            )
-            out[spot(ORDER1, yy * 4 + qq, core), M_OWN : M_OWN + 32, :] = part
-            for cc in range(2):
-                to_y = lax.bitwise_xor(jnp.int32(yy), 2 * cc + c // 4)
-                to = to_y * 4 + lax.bitwise_xor(jnp.int32(qq), c % 4)
-                lines = jnp.where(to < yy * 4 + qq, part[0:16].astype(F32), part[16:32].astype(F32))
-                first_row = M_TILE + 16 * cc
-                out[spot(ORDER1, to, core), first_row : first_row + 16, :] = lines.astype(BF16)
+        block[b, LIST : LIST + 32, :] = table
+    lists_out = pltpu.make_async_copy(
+        block.at[:, LIST:BLOCK1, :], out.at[:, LIST:BLOCK1, :], out_sems.at[1]
+    )
+    lists_out.start()
+    mon_out.wait()
+    lists_out.wait()
 
 
 def half_product(got, core):
@@ -319,9 +330,9 @@
         worst[8 * i : 8 * i + 8, :] = decode(block[0:8], block[9:10])
 
 
-def call(kernel, name, outs, *args, scratch=(), space=pltpu.VMEM, vmem_mib=24):
+def call(kernel, name, outs, *args, scratch=(), space=pltpu.VMEM, first=pltpu.VMEM, vmem_mib=24):
     vmem = pl.BlockSpec(memory_space=pltpu.VMEM)
-    specs = [vmem] * len(outs)
+    specs = [pl.BlockSpec(memory_space=first)] + [vmem] * (len(outs) - 1)
     shapes = [jax.ShapeDtypeStruct(s, d) for s, d in outs]
     many = len(outs) > 1
     return pl.pallas_call(
@@ -361,8 +372,9 @@
     scratch = [pltpu.SMEM(rows_used.shape, jnp.int32)]
     scratch += [pltpu.VMEM(a.shape, a.dtype) for a in inputs[1:8]]
     scratch += [pltpu.VMEM((32, ptdf_mon.shape[1]), BF16), pltpu.SemaphoreType.DMA((9,))]
+    scratch += [pltpu.VMEM((16, BLOCK1, 128), BF16), pltpu.SemaphoreType.DMA((2,))]
     block1 = call(
-        prep_kernel, "prep", [((16, BLOCK1, 128), BF16)], *inputs, scratch=scratch, space=pl.ANY, vmem_mib=60
+        prep_kernel, "prep", [((16, BLOCK1, 128), BF16)], *inputs, scratch=scratch, space=pl.ANY, first=pl.ANY, vmem_mib=60
     )
     groups1 = [
         [((n // 4) * 2 + core) * 4 + n % 4 for n in names]
@@ -425,7 +437,10 @@
         block3, ("cont", "core"), 0, 0, axis_index_groups=[group3], tiled=True
     )
     schur, worst_t = call(
-        place_kernel, "place", [((64, 2048), F32), ((64, 128), F32)], got3
+        place_kernel,
+        "place",
+        [((64, 2048), F32), ((64, 128), F32)],
+        got3,
     )
     return worst_t.T, schur
 

time: 70.3 us -> 70.2 us (level)
  no operation moved by 1% of the time
where the time goes in v6:
time: 70.2 us; the launch traced here: 69.7 us
  blocking collectives  36.1 us (51%)
  starting transfers between devices  15.2 us (22%)
  Pallas kernels  7.92 us (11%)
  waiting for transfers between devices  5.91 us (8%)
  other arithmetic  2.58 us (4%)
  between operations  1.61 us (2%)
    all_to_all x1, blocking collectives, local(): lax.all_to_all(block3, ('cont', 'core'), 0, 0, axis_index_groups=[group3]...  18.7 us
    all_to_all x1, blocking collectives, local(): lax.all_to_all(block2, ('cont', 'core'), 0, 0, axis_index_groups=groups2,...  17.4 us
    all_to_all x1, starting transfers between devices, local(): lax.all_to_all(block1, ('y', 'core', 'scen'), 0, 0, axis_index_groups=gro...  9.21 us
    pallas_call x6, Pallas kernels, call(): pl.pallas_call(kernel, name=name, out_shape=shapes if many else shapes[0]...  7.92 us
    ppermute x1, waiting for transfers between devices, local(): turned = lax.ppermute(turned, EVERY, pairs)  3.7 us
    ppermute x1, starting transfers between devices, local(): other1 = lax.ppermute(got1, 'core', [(0, 1), (1, 0)])  3.49 us
    reduce_max x1, other arithmetic, local(): jnp.max(terms, axis=2)  2.54 us
    ppermute x1, starting transfers between devices, local(): turned = lax.ppermute(turned, EVERY, pairs)  2.5 us
  transfers between devices with their start and end apart: 3, of which 2 were waited for; matrix products, arithmetic and copies ran while one was open for 4% of the time, Pallas kernels for 2%

profile of v6, /device:TPU:1, one launch (start us, length us, event | category | flops | bytes accessed | tf_op | source)
XLA Modules:
  0.0 69.7 jit_solution(14961332595431210997)
XLA Ops:
  0.6 0.0 copy-start.3
  0.6 0.0 copy-start.2
  0.7 0.0 copy-start.4
  0.7 0.0 copy-start
  1.5 2.6 %prep.1 = bf16[16,96,128]{2,1,0:T(8,128)(2,1)} custom-call(s32[1]{0:T(128)S(6)} %copy.18.refs_0_, s32[4,128]{1,0:T(4,128)} %bitcast.12, s32[4,128]{1,0:T(4,128)} %bitcast.13, s32[4,128]{1,0:T(4,128)} %bitcast.14, bf16[128,512]{1,0:T(8,128)(2,1)} %refs_4_.1, f32[64,128]{1,0:T(8,128)} %bitcast.11, f32[64,512]{1,0:T(8,128)} %refs_6_.1, f32[1,128]{1,0:T(1,128)} %bitcast.9, ...), custom_call_target="tpu_custom_call" | custom-call | tf_op jit(solution)/shard_map/prep/pallas_call | solution.py:338
  4.1 9.2 %all-to-all-start = ((bf16[16,96,128]{2,1,0:T(8,128)(2,1)}), bf16[16,96,128]{2,1,0:T(8,128)(2,1)S(1)}, u32[]{:S(2)}, u32[]{:S(2)}) async-start(bf16[16,96,128]{2,1,0:T(8,128)(2,1)} %prep.1), calls=%async_computation | async-start | bytes 786432 | tf_op jit(solution)/shard_map/all_to_all | solution.py:383
  13.3 0.0 copy-done.2
  13.3 0.0 copy-done.3
  13.3 2.5 %multiply_reduce_fusion.1 = (f32[64,128]{1,0:T(8,128)S(1)}, f32[64,128]{1,0:T(8,128)S(1)}) fusion(f32[64,512]{1,0:T(8,128)S(1)} %copy-done.3, f32[128,512]{1,0:T(8,128)S(1)} %convert_element_type.3), kind=kLoop, calls=%fused_computation.1 | loop fusion | flops 12566528 | bytes 458752 | tf_op jit(solution)/shard_map/reduce_max | solution.py:390
  15.9 0.0 copy-done
  15.9 0.2 constant_dynamic-slice_fusion.1
  16.1 0.1 copy.16
  16.2 0.1 copy.17
  16.3 0.0 copy-done.4
  16.3 0.0 copy-start.1
  16.3 2.2 %all-to-all-done.got.own = bf16[16,96,128]{2,1,0:T(8,128)(2,1)S(1)} async-done(((bf16[16,96,128]{2,1,0:T(8,128)(2,1)}), bf16[16,96,128]{2,1,0:T(8,128)(2,1)S(1)}, u32[]{:S(2)}, u32[]{:S(2)}) %all-to-all-start) | async-done | bytes 393248 | tf_op jit(solution)/shard_map/all_to_all | solution.py:383
  18.5 3.5 %collective-permute-start = (bf16[16,96,128]{2,1,0:T(8,128)(2,1)S(1)}, bf16[16,96,128]{2,1,0:T(8,128)(2,1)S(1)}, u32[]{:S(2)}, u32[]{:S(2)}) collective-permute-start(bf16[16,96,128]{2,1,0:T(8,128)(2,1)S(1)} %all-to-all-done.got.own), channel_id=1, source_target_pairs={{0,4},{4,0},{1,5},{5,1},{2,6},{6,2},{3,7},{7,3},{8,12},{12,8},{9,1... | collective-permute-start | bytes 1179656 | tf_op jit(solution)/shard_map/ppermute | solution.py:398
  22.0 1.6 %first.1 = (f32[128,512]{1,0:T(8,128)S(1)}, f32[8,128]{1,0:T(8,128)S(1)}) custom-call(bf16[16,96,128]{2,1,0:T(8,128)(2,1)S(1)} %all-to-all-done.got.own), custom_call_target="tpu_custom_call" | custom-call | tf_op jit(solution)/shard_map/first/pallas_call | solution.py:338
  23.6 0.0 collective-permute-done.got.other
  23.6 2.0 %second.1 = bf16[8,160,128]{2,1,0:T(8,128)(2,1)S(1)} custom-call(bf16[16,96,128]{2,1,0:T(8,128)(2,1)S(1)} %collective-permute-done.got.other, f32[128,512]{1,0:T(8,128)S(1)} %get-tuple-element.13.part1, f32[8,128]{1,0:T(8,128)S(1)} %get-tuple-element.14.sums1, bf16[512,2048]{1,0:T(8,128)(2,1)S(1)} %copy-done, ...), custom_call_target="tpu_custom_call" | custom-call | tf_op jit(solution)/shard_map/second/pallas_call | solution.py:338
  25.6 17.4 %all_to_all.15.got2 = bf16[8,160,128]{2,1,0:T(8,128)(2,1)S(1)} all-to-all(bf16[8,160,128]{2,1,0:T(8,128)(2,1)S(1)} %second.1), channel_id=1, replica_groups={{0,32,64,96,128,160,192,224},{132,164,196,228,4,36,68,100},{1,33,65,97,..., dimensions={0} | all-to-all | bytes 655360 | tf_op jit(solution)/shard_map/all_to_all | solution.py:407
  43.0 0.0 copy-done.1
  43.0 0.7 combine.1
  43.7 2.5 %collective-permute-start.1 = (s16[144,128]{1,0:T(8,128)(2,1)S(1)}, s16[144,128]{1,0:T(8,128)(2,1)S(1)}, u32[]{:S(2)}, u32[]{:S(2)}) collective-permute-start(s16[144,128]{1,0:T(8,128)(2,1)S(1)} %get-tuple-element.17), channel_id=1, source_target_pairs={{0,0},{1,1},{2,2},{3,3},{4,20},{5,21},{6,22},{7,23},{8,8},{9,9},{1... | collective-permute-start | bytes 110600 | tf_op jit(solution)/shard_map/ppermute | solution.py:428
  46.2 3.7 %collective-permute-done.1.turned = s16[144,128]{1,0:T(8,128)(2,1)S(1)} collective-permute-done((s16[144,128]{1,0:T(8,128)(2,1)S(1)}, s16[144,128]{1,0:T(8,128)(2,1)S(1)}, u32[]{:S(2)}, u32[]{:S(2)}) %collective-permute-start.1) | collective-permute-done | bytes 36896 | tf_op jit(solution)/shard_map/ppermute | solution.py:428
  49.9 0.1 finish.1
  49.9 18.7 %all_to_all.16.got = s16[16,80,128]{2,1,0:T(8,128)(2,1)S(1)} all-to-all(s16[16,80,128]{2,1,0:T(8,128)(2,1)S(1)} %finish.1), channel_id=1, replica_groups={{0,32,64,96,128,160,192,224,4,36,68,100,132,164,196,228},{1,33,65,97,12..., dimensions={0} | all-to-all | bytes 655360 | tf_op jit(solution)/shard_map/all_to_all | solution.py:436
  68.7 1.0 %place.1 = (f32[64,2048]{1,0:T(8,128)}, f32[64,128]{1,0:T(8,128)}) custom-call(s16[16,80,128]{2,1,0:T(8,128)(2,1)S(1)} %all_to_all.16.got), custom_call_target="tpu_custom_call" | custom-call | tf_op jit(solution)/shard_map/place/pallas_call | solution.py:338
  (3 shorter events, 0.0 us)
Async XLA Ops:
  0.6 12.7 %copy-start.3 = (f32[64,512]{1,0:T(8,128)S(1)}, f32[64,512]{1,0:T(8,128)}, u32[]{:S(2)}) copy-start(f32[64,512]{1,0:T(8,128)} %refs_6_.1) | copy-start | bytes 393220
  0.6 12.7 %copy-start.2 = (bf16[128,512]{1,0:T(8,128)(2,1)S(1)}, bf16[128,512]{1,0:T(8,128)(2,1)}, u32[]{:S(2)}) copy-start(bf16[128,512]{1,0:T(8,128)(2,1)} %refs_4_.1) | copy-start | bytes 393220
  0.7 15.6 %copy-start.4 = (f32[128,64]{0,1:T(8,128)S(1)}, f32[128,64]{0,1:T(8,128)}, u32[]{:S(2)}) copy-start(f32[128,64]{0,1:T(8,128)} %param.11) | copy-start | bytes 98308
  0.7 15.2 %copy-start = (bf16[512,2048]{1,0:T(8,128)(2,1)S(1)}, bf16[512,2048]{1,0:T(8,128)(2,1)}, u32[]{:S(2)}) copy-start(bf16[512,2048]{1,0:T(8,128)(2,1)} %out_rows.1) | copy-start | bytes 6291460
  4.1 14.5 %all-to-all-start = ((bf16[16,96,128]{2,1,0:T(8,128)(2,1)}), bf16[16,96,128]{2,1,0:T(8,128)(2,1)S(1)}, u32[]{:S(2)}, u32[]{:S(2)}) async-start(bf16[16,96,128]{2,1,0:T(8,128)(2,1)} %prep.1), calls=%async_computation | async-start | bytes 786432 | tf_op jit(solution)/shard_map/all_to_all | solution.py:383
  16.3 26.7 %copy-start.1 = (f32[128]{0:T(128)S(1)}, f32[128]{0:T(128)}, u32[]{:S(2)}) copy-start(f32[128]{0:T(128)} %param.13) | copy-start | bytes 1540
  18.5 5.1 %collective-permute-start = (bf16[16,96,128]{2,1,0:T(8,128)(2,1)S(1)}, bf16[16,96,128]{2,1,0:T(8,128)(2,1)S(1)}, u32[]{:S(2)}, u32[]{:S(2)}) collective-permute-start(bf16[16,96,128]{2,1,0:T(8,128)(2,1)S(1)} %all-to-all-done.got.own), channel_id=1, source_target_pairs={{0,4},{4,0},{1,5},{5,1},{2,6},{6,2},{3,7},{7,3},{8,12},{12,8},{9,1... | collective-permute-start | bytes 1179656 | tf_op jit(solution)/shard_map/ppermute | solution.py:398
  43.7 6.2 %collective-permute-start.1 = (s16[144,128]{1,0:T(8,128)(2,1)S(1)}, s16[144,128]{1,0:T(8,128)(2,1)S(1)}, u32[]{:S(2)}, u32[]{:S(2)}) collective-permute-start(s16[144,128]{1,0:T(8,128)(2,1)S(1)} %get-tuple-element.17), channel_id=1, source_target_pairs={{0,0},{1,1},{2,2},{3,3},{4,20},{5,21},{6,22},{7,23},{8,8},{9,9},{1... | collective-permute-start | bytes 110600 | tf_op jit(solution)/shard_map/ppermute | solution.py:428

commit v7 on v6

--- a/solution.py
+++ b/solution.py
@@ -320,11 +320,10 @@
             source_c = lax.bitwise_xor(jnp.int32(yy % 2), y % 2) * 4
             source_c = source_c + lax.bitwise_xor(jnp.int32(qq), q)
             source_core = lax.bitwise_xor(jnp.int32(yy // 2), y // 2)
-            block = got[spot3(source_c, source_core), :, :].astype(jnp.int32).astype(F32)
-            parts.append(decode(block[0:64], block[72:73]))
-        schur[:, 512 * yy : 512 * yy + 512] = jnp.concatenate(
-            [p[:, :64] for p in parts] + [p[:, 64:] for p in parts], axis=1
-        )
+            parts.append(got[spot3(source_c, source_core), :, :])
+        block = jnp.concatenate([p[:, :64] for p in parts] + [p[:, 64:] for p in parts], axis=1)
+        block = block.astype(jnp.int32).astype(F32)
+        schur[:, 512 * yy : 512 * yy + 512] = decode(block[0:64], block[72:73])
     for i in range(8):
         block = got[spot3(i, core), 64:80, :].astype(jnp.int32).astype(F32)
         worst[8 * i : 8 * i + 8, :] = decode(block[0:8], block[9:10])

time: 70.2 us -> 70.1 us (level)
  no operation moved by 1% of the time
where the time goes in v7:
time: 70.1 us; the launch traced here: 69.6 us
  blocking collectives  36.1 us (51%)
  starting transfers between devices  15.2 us (22%)
  Pallas kernels  7.87 us (11%)
  waiting for transfers between devices  5.91 us (8%)
  other arithmetic  2.58 us (4%)
  between operations  1.61 us (2%)
    all_to_all x1, blocking collectives, local(): lax.all_to_all(block3, ('cont', 'core'), 0, 0, axis_index_groups=[group3]...  18.7 us
    all_to_all x1, blocking collectives, local(): lax.all_to_all(block2, ('cont', 'core'), 0, 0, axis_index_groups=groups2,...  17.4 us
    all_to_all x1, starting transfers between devices, local(): lax.all_to_all(block1, ('y', 'core', 'scen'), 0, 0, axis_index_groups=gro...  9.21 us
    pallas_call x6, Pallas kernels, call(): pl.pallas_call(kernel, name=name, out_shape=shapes if many else shapes[0]...  7.87 us
    ppermute x1, waiting for transfers between devices, local(): turned = lax.ppermute(turned, EVERY, pairs)  3.7 us
    ppermute x1, starting transfers between devices, local(): other1 = lax.ppermute(got1, 'core', [(0, 1), (1, 0)])  3.49 us
    reduce_max x1, other arithmetic, local(): jnp.max(terms, axis=2)  2.54 us
    ppermute x1, starting transfers between devices, local(): turned = lax.ppermute(turned, EVERY, pairs)  2.5 us
  transfers between devices with their start and end apart: 3, of which 2 were waited for; matrix products, arithmetic and copies ran while one was open for 4% of the time, Pallas kernels for 2%

profile of v7, /device:TPU:1, one launch (start us, length us, event | category | flops | bytes accessed | tf_op | source)
XLA Modules:
  0.0 69.6 jit_solution(17881743790546553557)
XLA Ops:
  0.6 0.0 copy-start.3
  0.6 0.0 copy-start.2
  0.7 0.0 copy-start.4
  0.7 0.0 copy-start
  1.5 2.6 %prep.1 = bf16[16,96,128]{2,1,0:T(8,128)(2,1)} custom-call(s32[1]{0:T(128)S(6)} %copy.18.refs_0_, s32[4,128]{1,0:T(4,128)} %bitcast.12, s32[4,128]{1,0:T(4,128)} %bitcast.13, s32[4,128]{1,0:T(4,128)} %bitcast.14, bf16[128,512]{1,0:T(8,128)(2,1)} %refs_4_.1, f32[64,128]{1,0:T(8,128)} %bitcast.11, f32[64,512]{1,0:T(8,128)} %refs_6_.1, f32[1,128]{1,0:T(1,128)} %bitcast.9, ...), custom_call_target="tpu_custom_call" | custom-call | tf_op jit(solution)/shard_map/prep/pallas_call | solution.py:337
  4.1 9.2 %all-to-all-start = ((bf16[16,96,128]{2,1,0:T(8,128)(2,1)}), bf16[16,96,128]{2,1,0:T(8,128)(2,1)S(1)}, u32[]{:S(2)}, u32[]{:S(2)}) async-start(bf16[16,96,128]{2,1,0:T(8,128)(2,1)} %prep.1), calls=%async_computation | async-start | bytes 786432 | tf_op jit(solution)/shard_map/all_to_all | solution.py:382
  13.3 0.0 copy-done.2
  13.3 0.0 copy-done.3
  13.3 2.5 %multiply_reduce_fusion.1 = (f32[64,128]{1,0:T(8,128)S(1)}, f32[64,128]{1,0:T(8,128)S(1)}) fusion(f32[64,512]{1,0:T(8,128)S(1)} %copy-done.3, f32[128,512]{1,0:T(8,128)S(1)} %convert_element_type.3), kind=kLoop, calls=%fused_computation.1 | loop fusion | flops 12566528 | bytes 458752 | tf_op jit(solution)/shard_map/reduce_max | solution.py:389
  15.9 0.0 copy-done
  15.9 0.2 constant_dynamic-slice_fusion.1
  16.1 0.1 copy.16
  16.2 0.1 copy.17
  16.3 0.0 copy-done.4
  16.3 0.0 copy-start.1
  16.3 2.2 %all-to-all-done.got.own = bf16[16,96,128]{2,1,0:T(8,128)(2,1)S(1)} async-done(((bf16[16,96,128]{2,1,0:T(8,128)(2,1)}), bf16[16,96,128]{2,1,0:T(8,128)(2,1)S(1)}, u32[]{:S(2)}, u32[]{:S(2)}) %all-to-all-start) | async-done | bytes 393248 | tf_op jit(solution)/shard_map/all_to_all | solution.py:382
  18.5 3.5 %collective-permute-start = (bf16[16,96,128]{2,1,0:T(8,128)(2,1)S(1)}, bf16[16,96,128]{2,1,0:T(8,128)(2,1)S(1)}, u32[]{:S(2)}, u32[]{:S(2)}) collective-permute-start(bf16[16,96,128]{2,1,0:T(8,128)(2,1)S(1)} %all-to-all-done.got.own), channel_id=1, source_target_pairs={{0,4},{4,0},{1,5},{5,1},{2,6},{6,2},{3,7},{7,3},{8,12},{12,8},{9,1... | collective-permute-start | bytes 1179656 | tf_op jit(solution)/shard_map/ppermute | solution.py:397
  22.0 1.6 %first.1 = (f32[128,512]{1,0:T(8,128)S(1)}, f32[8,128]{1,0:T(8,128)S(1)}) custom-call(bf16[16,96,128]{2,1,0:T(8,128)(2,1)S(1)} %all-to-all-done.got.own), custom_call_target="tpu_custom_call" | custom-call | tf_op jit(solution)/shard_map/first/pallas_call | solution.py:337
  23.6 0.0 collective-permute-done.got.other
  23.6 2.0 %second.1 = bf16[8,160,128]{2,1,0:T(8,128)(2,1)S(1)} custom-call(bf16[16,96,128]{2,1,0:T(8,128)(2,1)S(1)} %collective-permute-done.got.other, f32[128,512]{1,0:T(8,128)S(1)} %get-tuple-element.13.part1, f32[8,128]{1,0:T(8,128)S(1)} %get-tuple-element.14.sums1, bf16[512,2048]{1,0:T(8,128)(2,1)S(1)} %copy-done, ...), custom_call_target="tpu_custom_call" | custom-call | tf_op jit(solution)/shard_map/second/pallas_call | solution.py:337
  25.6 17.4 %all_to_all.15.got2 = bf16[8,160,128]{2,1,0:T(8,128)(2,1)S(1)} all-to-all(bf16[8,160,128]{2,1,0:T(8,128)(2,1)S(1)} %second.1), channel_id=1, replica_groups={{0,32,64,96,128,160,192,224},{132,164,196,228,4,36,68,100},{1,33,65,97,..., dimensions={0} | all-to-all | bytes 655360 | tf_op jit(solution)/shard_map/all_to_all | solution.py:406
  43.0 0.0 copy-done.1
  43.0 0.7 combine.1
  43.7 2.5 %collective-permute-start.1 = (s16[144,128]{1,0:T(8,128)(2,1)S(1)}, s16[144,128]{1,0:T(8,128)(2,1)S(1)}, u32[]{:S(2)}, u32[]{:S(2)}) collective-permute-start(s16[144,128]{1,0:T(8,128)(2,1)S(1)} %get-tuple-element.17), channel_id=1, source_target_pairs={{0,0},{1,1},{2,2},{3,3},{4,20},{5,21},{6,22},{7,23},{8,8},{9,9},{1... | collective-permute-start | bytes 110600 | tf_op jit(solution)/shard_map/ppermute | solution.py:427
  46.2 3.7 %collective-permute-done.1.turned = s16[144,128]{1,0:T(8,128)(2,1)S(1)} collective-permute-done((s16[144,128]{1,0:T(8,128)(2,1)S(1)}, s16[144,128]{1,0:T(8,128)(2,1)S(1)}, u32[]{:S(2)}, u32[]{:S(2)}) %collective-permute-start.1) | collective-permute-done | bytes 36896 | tf_op jit(solution)/shard_map/ppermute | solution.py:427
  49.9 0.1 finish.1
  49.9 18.7 %all_to_all.16.got = s16[16,80,128]{2,1,0:T(8,128)(2,1)S(1)} all-to-all(s16[16,80,128]{2,1,0:T(8,128)(2,1)S(1)} %finish.1), channel_id=1, replica_groups={{0,32,64,96,128,160,192,224,4,36,68,100,132,164,196,228},{1,33,65,97,12..., dimensions={0} | all-to-all | bytes 655360 | tf_op jit(solution)/shard_map/all_to_all | solution.py:435
  68.7 1.0 %place.1 = (f32[64,2048]{1,0:T(8,128)}, f32[64,128]{1,0:T(8,128)}) custom-call(s16[16,80,128]{2,1,0:T(8,128)(2,1)S(1)} %all_to_all.16.got), custom_call_target="tpu_custom_call" | custom-call | tf_op jit(solution)/shard_map/place/pallas_call | solution.py:337
  (3 shorter events, 0.0 us)
Async XLA Ops:
  0.6 12.7 %copy-start.3 = (f32[64,512]{1,0:T(8,128)S(1)}, f32[64,512]{1,0:T(8,128)}, u32[]{:S(2)}) copy-start(f32[64,512]{1,0:T(8,128)} %refs_6_.1) | copy-start | bytes 393220
  0.6 12.7 %copy-start.2 = (bf16[128,512]{1,0:T(8,128)(2,1)S(1)}, bf16[128,512]{1,0:T(8,128)(2,1)}, u32[]{:S(2)}) copy-start(bf16[128,512]{1,0:T(8,128)(2,1)} %refs_4_.1) | copy-start | bytes 393220
  0.7 15.6 %copy-start.4 = (f32[128,64]{0,1:T(8,128)S(1)}, f32[128,64]{0,1:T(8,128)}, u32[]{:S(2)}) copy-start(f32[128,64]{0,1:T(8,128)} %param.11) | copy-start | bytes 98308
  0.7 15.2 %copy-start = (bf16[512,2048]{1,0:T(8,128)(2,1)S(1)}, bf16[512,2048]{1,0:T(8,128)(2,1)}, u32[]{:S(2)}) copy-start(bf16[512,2048]{1,0:T(8,128)(2,1)} %out_rows.1) | copy-start | bytes 6291460
  4.1 14.5 %all-to-all-start = ((bf16[16,96,128]{2,1,0:T(8,128)(2,1)}), bf16[16,96,128]{2,1,0:T(8,128)(2,1)S(1)}, u32[]{:S(2)}, u32[]{:S(2)}) async-start(bf16[16,96,128]{2,1,0:T(8,128)(2,1)} %prep.1), calls=%async_computation | async-start | bytes 786432 | tf_op jit(solution)/shard_map/all_to_all | solution.py:382
  16.3 26.7 %copy-start.1 = (f32[128]{0:T(128)S(1)}, f32[128]{0:T(128)}, u32[]{:S(2)}) copy-start(f32[128]{0:T(128)} %param.13) | copy-start | bytes 1540
  18.5 5.1 %collective-permute-start = (bf16[16,96,128]{2,1,0:T(8,128)(2,1)S(1)}, bf16[16,96,128]{2,1,0:T(8,128)(2,1)S(1)}, u32[]{:S(2)}, u32[]{:S(2)}) collective-permute-start(bf16[16,96,128]{2,1,0:T(8,128)(2,1)S(1)} %all-to-all-done.got.own), channel_id=1, source_target_pairs={{0,4},{4,0},{1,5},{5,1},{2,6},{6,2},{3,7},{7,3},{8,12},{12,8},{9,1... | collective-permute-start | bytes 1179656 | tf_op jit(solution)/shard_map/ppermute | solution.py:397
  43.7 6.2 %collective-permute-start.1 = (s16[144,128]{1,0:T(8,128)(2,1)S(1)}, s16[144,128]{1,0:T(8,128)(2,1)S(1)}, u32[]{:S(2)}, u32[]{:S(2)}) collective-permute-start(s16[144,128]{1,0:T(8,128)(2,1)S(1)} %get-tuple-element.17), channel_id=1, source_target_pairs={{0,0},{1,1},{2,2},{3,3},{4,20},{5,21},{6,22},{7,23},{8,8},{9,9},{1... | collective-permute-start | bytes 110600 | tf_op jit(solution)/shard_map/ppermute | solution.py:427
